TPU v7x, 256 devices: a whole 4x4x8 slice. The times are simulated.
256 devices in a mesh: row: 8 (over y, core), col: 8 (over x, z_lo), aux: 4 (over z_hi).
Axes of the slice: x: 4, y: 4, z: 8 (z_hi: 4, z_lo: 2; z = z_hi * 2 + z_lo), core: 2. Of those that a mesh axis runs over, the one named last changes fastest.
Arguments:
- slabs: bfloat16 [5056, 32, 512], P('row', 'col', 'aux'), may hold values from -6 to 6
- gammas: bfloat16 [5056, 32, 512], P('row', 'col', 'aux'), may hold values from -0.046875 to 0.046875
- occupied: int32 [5056], replicated, may hold values 0 or 1
- energies: float32 [5056], replicated, may hold values from -2 to 2
Outputs:
- gradient: float32 [5056, 5056], P(('row', 'aux'), 'col')
- rotation_step: float32 [5056, 5056], P(('row', 'aux'), 'col')
All inputs are finite; a program needn't handle non-finite values.
Results may differ from a plain program's by a relative error of at most 0.0003.
Values may be sent and summed in bfloat16 or wider, within the bound.
A program may use at most 128 MiB of HBM per device.

v0:
```python
import jax
import jax.numpy as jnp
from jax import lax
from jax.sharding import PartitionSpec as P


def on_device(slabs, gammas, occupied, energies):
    n_row = lax.axis_size("row")
    n_col = lax.axis_size("col")
    n_aux = lax.axis_size("aux")
    block_rows = slabs.shape[0]
    sub_rows = block_rows // n_aux
    total_orbs = block_rows * n_row
    col_block = total_orbs // n_col
    flat_slabs = slabs.reshape(block_rows, -1)
    piece = lax.all_gather(gammas, "row", axis=0, tiled=True)
    flat_piece = piece.reshape(piece.shape[0], -1)
    partial_value = jnp.dot(flat_slabs, flat_piece.T, preferred_element_type=jnp.float32)
    reduced = lax.psum_scatter(partial_value, "aux", scatter_dimension=0, tiled=True)
    arrived = lax.all_to_all(reduced, ("row", "aux"), split_axis=1, concat_axis=0, tiled=True)
    difference = reduced - arrived.T
    gradient = 2.0 * lax.psum_scatter(difference, "col", scatter_dimension=1, tiled=True)
    row_start = (lax.axis_index("row") * n_aux + lax.axis_index("aux")) * sub_rows
    col_start = lax.axis_index("col") * col_block
    energy_rows = lax.dynamic_slice_in_dim(energies, row_start, sub_rows)
    energy_cols = lax.dynamic_slice_in_dim(energies, col_start, col_block)
    occ_rows = lax.dynamic_slice_in_dim(occupied, row_start, sub_rows)
    occ_cols = lax.dynamic_slice_in_dim(occupied, col_start, col_block)
    nonredundant = occ_rows[:, None] + occ_cols[None, :] - 2 * occ_rows[:, None] * occ_cols[None, :]
    denominator = 4.0 * jnp.abs(energy_rows[:, None] - energy_cols[None, :]) + 0.5
    rotation_step = -nonredundant.astype(jnp.float32) * gradient / denominator
    return (gradient, rotation_step)


def solution(mesh):
    placed = (P("row", "col", "aux"), P("row", "col", "aux"), P(), P())
    return jax.shard_map(
        on_device,
        mesh=mesh,
        in_specs=placed,
        out_specs=(P(("row", "aux"), "col"), P(("row", "aux"), "col")),
        check_vma=False,
    )
```

profile of v0, /device:TPU:4, one launch (start us, length us, event | category | flops | bytes accessed | tf_op | source)
XLA Modules:
  0.0 651.3 jit_solution(12018909124603307763)
XLA Ops:
  7.2 0.0 all-gather.2.cloned.1.call-start
  7.2 2.0 copy.9
  9.2 0.0 all-gather.2.cloned.1.call-update
  9.2 0.0 reduce-scatter.6.cloned.1.call-start
  9.3 42.3 %all-gather.2.cloned.1.call-done = bf16[5056,4,128]{2,0,1:T(8,128)(2,1)} async-done(((bf16[632,4,128]{2,0,1:T(8,128)(2,1)}), bf16[5056,4,128]{2,0,1:T(8,128)(2,1)}) %all-gather.2.cloned.1.call-update) | async-done | bytes 5177360 | tf_op jit(solution)/shard_map/all_gather | solution.py:16
  51.6 10.9 %convolution_bitcast_fusion = f32[632,5056]{1,0:T(8,128)} fusion(bf16[5056,4,128]{2,0,1:T(8,128)(2,1)} %all-gather.2.cloned.1.call-done, bf16[632,4,128]{2,1,0:T(4,128)(2,1)} %param.4), kind=kOutput, calls=%fused_computation | convolution fusion | flops 3272081408 | bytes 18606080 | tf_op jit(solution)/shard_map/dot_general | solution.py:18
  62.5 0.0 copy-start.1
  62.5 294.9 %fusion = f32[160,5056]{1,0:T(8,128)S(1)} fusion(f32[632,5056]{1,0:T(8,128)} %convolution_bitcast_fusion), kind=kCustom, calls=%all-reduce-scatter | all-reduce-scatter fusion | flops 3235841 | bytes 16018432
  357.4 0.0 copy-start
  357.4 3.6 collective-permute-start
  361.0 0.0 copy-done.1
  361.0 0.6 dynamic-slice.4
  362.2 0.0 copy-done
  362.2 1.1 collective-permute-done
  363.3 9.1 %concatenate = f32[166,5056]{1,0:T(8,128)S(1)} concatenate(f32[6,5056]{1,0:T(8,128)} %collective-permute-done, f32[160,5056]{1,0:T(8,128)} %copy-done), dimensions={0} | concatenate | bytes 6714368
  372.4 2.1 constant_dynamic-slice_fusion
  374.5 9.2 %all_to_all.14 = f32[158,32,158]{2,1,0:T(8,128)} reshape(f32[158,5056]{1,0:T(8,128)} %constant_dynamic-slice_fusion) | data formatting | bytes 6390784 | tf_op jit(solution)/shard_map/all_to_all | solution.py:20
  383.6 6.4 copy.11
  390.1 122.2 %all_to_all.19 = f32[158,32,158]{0,2,1:T(8,128)S(1)} all-to-all(f32[158,32,158]{0,2,1:T(8,128)} %copy.11), channel_id=1, replica_groups=mesh['row'=8,'col'=8,'aux'=4] {'row','aux'}, dimensions={1} | all-to-all | bytes 6390784 | tf_op jit(solution)/shard_map/all_to_all | solution.py:20
  512.3 5.3 copy.12
  517.6 5.9 all_to_all.17
  523.5 4.0 bitcast_subtract_fusion
  527.5 5.4 copy.13
  533.0 0.0 reduce-scatter.6.cloned.1.call-update
  533.0 0.8 dynamic_slice.14
  533.8 0.8 dynamic_slice.15
  534.6 0.8 dynamic_slice.13
  535.3 0.8 broadcast_multiply_fusion.1
  536.1 105.9 %reduce-scatter.6.cloned.1.call-done = f32[632,158]{1,0:T(8,128)} async-done(((f32[5056,158]{1,0:T(8,128)}), f32[632,158]{1,0:T(8,128)}) %reduce-scatter.6.cloned.1.call-update) | async-done | bytes 399440
  642.0 1.3 copy.14
  643.3 1.1 add_divide_fusion
  (1 shorter events, 0.0 us)
Async XLA Ops:
  7.2 44.4 %all-gather.2.cloned.1.call-start = ((), (), s32[]{:S(2)}) async-start(), calls=%async_computation.2 | async-start | bytes 5824512 | tf_op jit(solution)/shard_map/all_gather | solution.py:16
  9.2 632.8 %reduce-scatter.6.cloned.1.call-start = ((), (), s32[]{:S(2)}) async-start(), calls=%async_computation.3 | async-start | bytes 5824512
  62.5 298.5 %copy-start.1 = (u32[256]{0:T(256)S(1)}, u32[256]{0:T(256)}, u32[]{:S(2)}) copy-start(u32[256]{0:T(256)} %constant.35) | copy-start | bytes 3076
  357.4 4.8 copy-start
  357.4 5.9 collective-permute-start
Sparse Core Ops, SparseCore 0:
  9.8 41.7 all-gather.1
  533.1 108.8 reduce-scatter.5
where the time goes:
time: 654 us; the launch traced here: 651 us
  blocking collectives  417 us (64%)
  waiting for transfers between devices  149 us (23%)
  local copies, waits for them, and re-layouts  49.7 us (8%)
  between operations  14.7 us (2%)
  matrix products  10.9 us (2%)
    unnamed x1, blocking collectives  295 us
    all_to_all x1, blocking collectives, on_device(): lax.all_to_all(reduced, ('row', 'aux'), split_axis=1, concat_axis=0, tile...  122 us
    unnamed x4, waiting for transfers between devices  107 us
    all_gather x1, waiting for transfers between devices, on_device(): piece = lax.all_gather(gammas, 'row', axis=0, tiled=True)  42.3 us
    all_to_all x4, local copies, waits for them, and re-layouts, on_device(): lax.all_to_all(reduced, ('row', 'aux'), split_axis=1, concat_axis=0, tile...  26.8 us
    unnamed x11, local copies, waits for them, and re-layouts  20.5 us
  transfers between devices with their start and end apart: 3, of which 3 were waited for; matrix products, arithmetic and copies ran while one was open for 1% of the time, Pallas kernels for 0%

commit v1 on v0

v1 whole, which is shorter than its diff:
```python
import functools

import jax
import jax.numpy as jnp
from jax import lax
from jax.experimental import pallas as pl
from jax.experimental.pallas import tpu as pltpu
from jax.sharding import PartitionSpec as P

SUB = 160
STEPS = 2
CH = SUB // STEPS
HALF = CH // 2
WIDE = 4 * SUB
KX = 512
PIECE = 256


def kernel(s_ref, g_ref, direct, mirror, sbuf, gbuf, fock, rs_half, rs_full, send, recv, loc):
    row, col, aux = lax.axis_index("row"), lax.axis_index("col"), lax.axis_index("aux")
    y, c = row // 2, row % 2
    x, zlo = col // 2, col % 2
    z = 2 * aux + zlo

    def at(row_=row, col_=col, aux_=aux):
        return {"row": row_, "col": col_, "aux": aux_}

    def x_at(d):
        return at(col_=2 * ((x + d) % 4) + zlo)

    def y_at(d):
        return at(row_=2 * ((y + d) % 4) + c)

    def z_at(d):
        there = (z + d) % 8
        return at(col_=2 * x + there % 2, aux_=there // 2)

    other = at(row_=2 * y + (1 - c))

    sends = []
    count = [0]

    def slot():
        count[0] += 1
        return count[0] - 1

    def put(n, src, dst, dev):
        copy = pltpu.make_async_remote_copy(
            src_ref=src, dst_ref=dst, send_sem=send.at[n], recv_sem=recv.at[n],
            device_id=dev, device_id_type=pl.DeviceIdType.MESH)
        copy.start()
        sends.append(copy)

    def got(n, dst, dev):
        pltpu.make_async_remote_copy(
            src_ref=dst, dst_ref=dst, send_sem=send.at[n], recv_sem=recv.at[n],
            device_id=dev, device_id_type=pl.DeviceIdType.MESH).wait_recv()

    def mirror_from(r):
        return at(2 * x + zlo, 2 * aux + c, r)

    def mirror_to(t):
        return at(2 * t + zlo, 2 * y + c, x)

    on_diagonal = jnp.logical_and(jnp.logical_and(zlo == c, x == y), aux == x)

    barrier = pltpu.get_barrier_semaphore()

    def greet(dev):
        pl.semaphore_signal(barrier, inc=1, device_id=dev, device_id_type=pl.DeviceIdType.MESH)

    for dev in (x_at(1), x_at(3), x_at(2), y_at(1), y_at(3), other, z_at(1), z_at(7)):
        greet(dev)
    for r in range(4):
        mine = jnp.logical_and(on_diagonal, aux == r)

        @pl.when(jnp.logical_not(mine))
        def _():
            greet(mirror_from(r))

    pl.semaphore_wait(barrier, 12 - on_diagonal.astype(jnp.int32))

    lanes = [pl.ds(KX * p, KX) for p in range(4)]

    a2a = [None] + [slot() for _ in range(3)]
    for d in (1, 3, 2):
        put(a2a[d], g_ref.at[(x + d) % 4], gbuf.at[c, y, :, lanes[(4 - d) % 4]], x_at(d))
    gbuf[c, y, :, 0:KX] = g_ref[x]

    s_plus = [slot() for _ in range(STEPS)]
    s_minus = [slot() for _ in range(STEPS)]
    s_fwd = [[slot(), slot()] for _ in range(STEPS)]
    rows_half = 2 * CH

    def send_rows(h):
        put(s_plus[h], s_ref.at[h], sbuf.at[h, :, lanes[3]], x_at(1))
        put(s_minus[h], s_ref.at[h], sbuf.at[h, :, lanes[1]], x_at(3))

    def forward_rows(h):
        low, high = pl.ds(0, rows_half), pl.ds(rows_half, rows_half)
        got(s_plus[h], sbuf.at[h, :, lanes[3]], x_at(3))
        put(s_fwd[h][0], sbuf.at[h, low, lanes[3]], sbuf.at[h, low, lanes[2]], x_at(1))
        got(s_minus[h], sbuf.at[h, :, lanes[1]], x_at(1))
        put(s_fwd[h][1], sbuf.at[h, high, lanes[1]], sbuf.at[h, high, lanes[2]], x_at(3))

    def finish_rows(h):
        low, high = pl.ds(0, rows_half), pl.ds(rows_half, rows_half)
        got(s_fwd[h][0], sbuf.at[h, low, lanes[2]], x_at(3))
        got(s_fwd[h][1], sbuf.at[h, high, lanes[2]], x_at(1))

    y_plus = [slot() for _ in range(4)]
    y_minus = [slot() for _ in range(4)]
    y_far = [slot() for _ in range(4)]
    cross = [[slot() for _ in range(4)] for _ in range(4)]

    def piece(core, yy, p):
        return gbuf.at[core, yy, :, lanes[p]]

    def over(d, p):
        yy = (y + d) % 4
        put(cross[d][p], piece(c, yy, p), piece(c, yy, p), other)

    def spread(p):
        put(y_plus[p], piece(c, y, p), piece(c, y, p), y_at(1))
        put(y_minus[p], piece(c, y, p), piece(c, y, p), y_at(3))
        over(0, p)

    def relay(p):
        below, above = (y + 3) % 4, (y + 1) % 4
        got(y_plus[p], piece(c, below, p), y_at(3))
        if p in (0, 1):
            put(y_far[p], piece(c, below, p), piece(c, below, p), y_at(1))
        over(3, p)
        got(y_minus[p], piece(c, above, p), y_at(1))
        if p in (2, 3):
            put(y_far[p], piece(c, above, p), piece(c, above, p), y_at(3))
        over(1, p)

    def relay_far(p):
        got(y_far[p], piece(c, (y + 2) % 4, p), y_at(3) if p in (0, 1) else y_at(1))
        over(2, p)

    spread(0)
    for h in range(STEPS):
        send_rows(h)
        sbuf[h, :, 0:KX] = s_ref[h]
    for d in (1, 3, 2):
        p = (4 - d) % 4
        got(a2a[d], piece(c, y, p), x_at(4 - d))
        spread(p)
    relay(0)
    relay(3)
    relay(1)
    forward_rows(0)
    relay(2)
    for p in (0, 3, 1, 2):
        relay_far(p)
    for d in range(4):
        for p in range(4):
            got(cross[d][p], piece(1 - c, (y + d) % 4, p), other)

    rs_send = [[[slot() for _ in range(4)] for _ in range(2)] for _ in range(STEPS)]

    def multiply(h):
        def column_block(cc, carry):
            out = lax.dot_general(
                sbuf[h], gbuf[cc].reshape(WIDE, 4 * KX), (((1,), (1,)), ((), ())),
                preferred_element_type=jnp.float32)
            fock[h, :, cc] = out.reshape(4, CH, WIDE)
            return carry

        lax.fori_loop(0, 2, column_block, 0)

    def chunk(h, d):
        there = (z + d) % 8
        return h, there // 2, there % 2

    halves = (pl.ds(0, HALF), pl.ds(HALF, HALF))

    def reduce_step(h, t):
        for way in range(2):
            sign = 1 if way == 0 else 7
            nxt, prev = z_at(sign), z_at(8 - sign)
            here = chunk(h, sign * (4 - t))
            if t == 0:
                put(rs_send[h][way][0], fock.at[(*here, halves[way])], rs_half.at[way, h], nxt)
                continue
            if t == 1:
                got(rs_send[h][way][0], rs_half.at[way, h], prev)
                fock[(*here, halves[way])] += rs_half[way, h]
            else:
                got(rs_send[h][way][t - 1], rs_full.at[way, h, t - 2], prev)
                fock[here] += rs_full[way, h, t - 2]
            if t < 4:
                put(rs_send[h][way][t], fock.at[here], rs_full.at[way, h, t - 1], nxt)

    for h in range(STEPS):
        if h > 0:
            forward_rows(h)
        finish_rows(h)
        multiply(h)
        reduce_step(h, 0)
    for t in range(1, 5):
        for h in range(STEPS):
            reduce_step(h, t)

    x_out = [[slot() for _ in range(3)] for _ in range(STEPS)]
    m_out = [[slot() for _ in range(4)] for _ in range(STEPS)]
    for h in range(STEPS):
        rows = pl.ds(CH * h, CH)
        mine = fock.at[h, aux, zlo]

        def lanes_of(t):
            return pl.ds(pl.multiple_of(128 * t, 128), PIECE)

        for d in (1, 2, 3):
            put(x_out[h][d - 1], mine.at[:, lanes_of((x + d) % 4)], direct.at[x, rows], x_at(d))
        for t in range(4):
            copy_args = (mine.at[:, lanes_of(t)], mirror.at[aux, rows])
            here = jnp.logical_and(on_diagonal, y == t)

            @pl.when(here)
            def _():
                local = pltpu.make_async_copy(*copy_args, loc.at[STEPS + h])
                local.start()
                local.wait()

            @pl.when(jnp.logical_not(here))
            def _():
                pltpu.make_async_remote_copy(
                    src_ref=copy_args[0], dst_ref=copy_args[1],
                    send_sem=send.at[m_out[h][t]], recv_sem=recv.at[m_out[h][0] + aux],
                    device_id=mirror_to(t), device_id_type=pl.DeviceIdType.MESH).start()
        local = pltpu.make_async_copy(mine.at[:, lanes_of(x)], direct.at[x, rows], loc.at[h])
        local.start()
        local.wait()

    for h in range(STEPS):
        rows = pl.ds(CH * h, CH)
        for d in (1, 2, 3):
            got(x_out[h][d - 1], direct.at[(x + 4 - d) % 4, rows], x_at(4 - d))
        for r in range(4):
            @pl.when(jnp.logical_not(jnp.logical_and(on_diagonal, aux == r)))
            def _():
                got(m_out[h][r], mirror.at[r, rows], mirror_from(r))

    for copy in sends:
        copy.wait_send()
    for h in range(STEPS):
        rows = pl.ds(CH * h, CH)
        for t in range(4):
            @pl.when(jnp.logical_not(jnp.logical_and(on_diagonal, y == t)))
            def _():
                pltpu.make_async_remote_copy(
                    src_ref=fock.at[h, aux, zlo, :, pl.ds(0, PIECE)], dst_ref=mirror.at[aux, rows],
                    send_sem=send.at[m_out[h][t]], recv_sem=recv.at[m_out[h][0] + aux],
                    device_id=mirror_to(t), device_id_type=pl.DeviceIdType.MESH).wait_send()


COPIES = 3 + 4 * STEPS + 12 + 16 + 8 * STEPS + 7 * STEPS


def exchange(slabs, gammas):
    vmem = pl.BlockSpec(memory_space=pltpu.VMEM)
    out = jax.ShapeDtypeStruct((4, SUB, PIECE), jnp.float32)
    return pl.pallas_call(
        kernel,
        out_shape=(out, out),
        in_specs=[vmem, vmem],
        out_specs=(vmem, vmem),
        scratch_shapes=[
            pltpu.VMEM((STEPS, 4 * CH, 4 * KX), jnp.bfloat16),
            pltpu.VMEM((2, 4, SUB, 4 * KX), jnp.bfloat16),
            pltpu.VMEM((STEPS, 4, 2, CH, WIDE), jnp.float32),
            pltpu.VMEM((2, STEPS, HALF, WIDE), jnp.float32),
            pltpu.VMEM((2, STEPS, 3, CH, WIDE), jnp.float32),
            pltpu.SemaphoreType.DMA((COPIES,)),
            pltpu.SemaphoreType.DMA((COPIES,)),
            pltpu.SemaphoreType.DMA((2 * STEPS,)),
        ],
        compiler_params=pltpu.CompilerParams(
            collective_id=0, has_side_effects=True, vmem_limit_bytes=48 * 1024 * 1024),
        cost_estimate=pl.CostEstimate(
            flops=2 * 640 * 1280 * 2048, bytes_accessed=4 * 1024 * 1024, transcendentals=0),
    )(slabs, gammas)


def on_device(slabs, gammas, occupied, energies):
    block = slabs.shape[0]
    sub = block // 4

    def pieces(a):
        return jnp.pad(a.reshape(4, sub, KX), ((0, 0), (0, SUB - sub), (0, 0)))

    row, col, aux = lax.axis_index("row"), lax.axis_index("col"), lax.axis_index("aux")
    s = pieces(slabs).reshape(4, STEPS, CH, KX).transpose(1, 0, 2, 3).reshape(STEPS, 4 * CH, KX)
    direct, mirror = exchange(s, pieces(gammas))
    own = lax.dynamic_slice_in_dim(direct[:, :sub], 32 * (col // 2), sub, axis=2)
    other = lax.dynamic_slice_in_dim(mirror[:, :sub], 32 * (row // 2), sub, axis=2)
    own = own.transpose(1, 0, 2).reshape(sub, block)
    other = other.reshape(block, sub).T
    gradient = 2.0 * (own - other)
    row_start = row * block + aux * sub
    col_start = col * block
    energy_rows = lax.dynamic_slice_in_dim(energies, row_start, sub)
    energy_cols = lax.dynamic_slice_in_dim(energies, col_start, block)
    occ_rows = lax.dynamic_slice_in_dim(occupied, row_start, sub)
    occ_cols = lax.dynamic_slice_in_dim(occupied, col_start, block)
    nonredundant = occ_rows[:, None] + occ_cols[None, :] - 2 * occ_rows[:, None] * occ_cols[None, :]
    denominator = 4.0 * jnp.abs(energy_rows[:, None] - energy_cols[None, :]) + 0.5
    rotation_step = -nonredundant.astype(jnp.float32) * gradient / denominator
    return (gradient, rotation_step)


def solution(mesh):
    placed = (P("row", "col", "aux"), P("row", "col", "aux"), P(), P())
    return jax.shard_map(
        on_device,
        mesh=mesh,
        in_specs=placed,
        out_specs=(P(("row", "aux"), "col"), P(("row", "aux"), "col")),
        check_vma=False,
    )
```

time: 654 us -> 155 us (0.24)
  blocking collectives: 417 us -> 0 us
  waiting for transfers between devices: 149 us -> 0 us
  Pallas kernels: 0 us -> 142 us
  local copies, waits for them, and re-layouts: 49.7 us -> 6.63 us
  between operations: 14.7 us -> 0.74 us
  matrix products: 10.9 us -> 0 us
    unnamed x1 -> x0, blocking collectives: 295 us -> none
    pallas_call x0 -> x1, Pallas kernels: none -> 142 us  [exchange(): pl.pallas_call(kernel, out_shape=(out, out), in_specs=[vmem, vmem], out_s...]
    all_to_all x1 -> x0, blocking collectives: 122 us -> none  [on_device(): lax.all_to_all(reduced, ('row', 'aux'), split_axis=1, concat_axis=0, tile...]
    unnamed x4 -> x0, waiting for transfers between devices: 107 us -> none
    all_gather x1 -> x0, waiting for transfers between devices: 42.3 us -> none  [on_device(): piece = lax.all_gather(gammas, 'row', axis=0, tiled=True)]
    all_to_all x4 -> x0, local copies, waits for them, and re-layouts: 26.8 us -> none  [on_device(): lax.all_to_all(reduced, ('row', 'aux'), split_axis=1, concat_axis=0, tile...]
    unnamed x11 -> x2, local copies, waits for them, and re-layouts: 20.5 us -> 1.03 us
    dot_general x1 -> x0, matrix products: 10.9 us -> none  [on_device(): jnp.dot(flat_slabs, flat_piece.T, preferred_element_type=jnp.float32)]
  transfers between devices with their start and end apart: 3 -> 0, of which waited for: 3 -> 0; matrix products, arithmetic and copies ran while one was open for 1% -> 0% of each run, Pallas kernels for 0% -> 0%
where the time goes in v1:
time: 155 us; the launch traced here: 152 us
  Pallas kernels  142 us (92%)
  local copies, waits for them, and re-layouts  6.63 us (4%)
  other arithmetic  1.91 us (1%)
    pallas_call x1, Pallas kernels, exchange(): pl.pallas_call(kernel, out_shape=(out, out), in_specs=[vmem, vmem], out_s...  142 us

profile of v1, /device:TPU:4, one launch (start us, length us, event | category | flops | bytes accessed | tf_op | source)
XLA Modules:
  0.0 151.7 jit_solution(9872602402363209998)
XLA Ops:
  0.7 1.3 reshape.28
  2.0 0.1 pad.7
  2.0 0.0 copy-start
  2.1 1.0 copy-done
  3.1 0.2 reshape.31
  3.4 0.1 pad.8.g_ref
  3.4 142.5 %shard_map.59 = (f32[4,160,256]{2,1,0:T(8,128)S(1)}, f32[4,160,256]{2,1,0:T(8,128)S(1)}) custom-call(bf16[2,320,512]{2,1,0:T(8,128)(2,1)S(1)} %bitcast.14, bf16[4,160,512]{2,1,0:T(8,128)(2,1)S(1)} %pad.8.g_ref), custom_call_target="tpu_custom_call" | custom-call | flops 3355443200 | bytes 4194304 | tf_op jit(solution)/shard_map/pallas_call | solution.py:266
  145.9 0.2 constant_dynamic-slice_fusion
  146.2 0.1 reshape.34
  146.2 0.2 copy.9
  146.4 0.2 dynamic-slice_bitcast_fusion
  146.7 0.4 copy.7
  147.1 0.4 reshape.32
  147.5 0.8 broadcast_multiply_fusion
  148.3 0.8 dynamic_slice.22
  149.1 0.8 dynamic_slice.21
  149.8 0.8 dynamic_slice.23
  150.6 1.1 add_divide_fusion
  (1 shorter events, 0.0 us)
Async XLA Ops:
  2.0 1.1 copy-start

commit v2 on v1

--- a/solution.py
+++ b/solution.py
@@ -16,7 +16,7 @@
 PIECE = 256
 
 
-def kernel(s_ref, g_ref, direct, mirror, sbuf, gbuf, fock, rs_half, rs_full, send, recv, loc):
+def kernel(s_ref, g_ref, direct, mirror, sbuf, gbuf, fock, rs_half, rs_full, by_y, by_x, send, recv, loc):
     row, col, aux = lax.axis_index("row"), lax.axis_index("col"), lax.axis_index("aux")
     y, c = row // 2, row % 2
     x, zlo = col // 2, col % 2
@@ -56,29 +56,24 @@
             src_ref=dst, dst_ref=dst, send_sem=send.at[n], recv_sem=recv.at[n],
             device_id=dev, device_id_type=pl.DeviceIdType.MESH).wait_recv()
 
-    def mirror_from(r):
-        return at(2 * x + zlo, 2 * aux + c, r)
-
-    def mirror_to(t):
-        return at(2 * t + zlo, 2 * y + c, x)
-
-    on_diagonal = jnp.logical_and(jnp.logical_and(zlo == c, x == y), aux == x)
+    def swapped(m):
+        return at(2 * y + zlo, 2 * x + c, m)
+
+    same_core = zlo == c
 
     barrier = pltpu.get_barrier_semaphore()
 
     def greet(dev):
         pl.semaphore_signal(barrier, inc=1, device_id=dev, device_id_type=pl.DeviceIdType.MESH)
 
-    for dev in (x_at(1), x_at(3), x_at(2), y_at(1), y_at(3), other, z_at(1), z_at(7)):
+    for dev in (x_at(1), x_at(3), x_at(2), y_at(1), y_at(3), y_at(2), other, z_at(1), z_at(7)):
         greet(dev)
     for r in range(4):
-        mine = jnp.logical_and(on_diagonal, aux == r)
-
-        @pl.when(jnp.logical_not(mine))
+        @pl.when(jnp.logical_not(jnp.logical_and(same_core, aux == r)))
         def _():
-            greet(mirror_from(r))
-
-    pl.semaphore_wait(barrier, 12 - on_diagonal.astype(jnp.int32))
+            greet(swapped(r))
+
+    pl.semaphore_wait(barrier, 13 - same_core.astype(jnp.int32))
 
     lanes = [pl.ds(KX * p, KX) for p in range(4)]
 
@@ -200,64 +195,113 @@
         finish_rows(h)
         multiply(h)
         reduce_step(h, 0)
+    x_out = [[slot() for _ in range(3)] for _ in range(STEPS)]
+    y_out = [[slot() for _ in range(3)] for _ in range(STEPS)]
+    t_out = [[slot() for _ in range(4)] for _ in range(STEPS)]
+    m_out = [[slot() for _ in range(4)] for _ in range(STEPS)]
+
+    def rows_of(h):
+        return pl.ds(CH * h, CH)
+
+    def lanes_of(t):
+        return pl.ds(pl.multiple_of(128 * t, 128), PIECE)
+
+    def local(n, src, dst):
+        return pltpu.make_async_copy(src, dst, loc.at[n])
+
+    def remote(n_send, n_recv, src, dst, dev):
+        return pltpu.make_async_remote_copy(
+            src_ref=src, dst_ref=dst, send_sem=send.at[n_send], recv_sem=recv.at[n_recv],
+            device_id=dev, device_id_type=pl.DeviceIdType.MESH)
+
+    def leave(h):
+        mine = fock.at[h, aux, zlo]
+        for d in (2, 1, 3):
+            put(y_out[h][d - 1], mine.at[:, lanes_of((y + d) % 4)], by_y.at[h, y], y_at(d))
+        for d in (2, 1, 3):
+            put(x_out[h][d - 1], mine.at[:, lanes_of((x + d) % 4)], direct.at[x, rows_of(h)], x_at(d))
+        copies = (local(4 * h, mine.at[:, lanes_of(y)], by_y.at[h, y]),
+                  local(4 * h + 1, mine.at[:, lanes_of(x)], direct.at[x, rows_of(h)]))
+        for copy in copies:
+            copy.start()
+        for copy in copies:
+            copy.wait()
+
+    def along_x(h, d):
+        t = (y + d) % 4
+        return remote(t_out[h][d], t_out[h][0] + x, by_y.at[h, t], by_x.at[h, x], at(col_=2 * t + zlo))
+
+    def along_z(h, m):
+        return remote(m_out[h][m], m_out[h][0] + aux, by_x.at[h, m], mirror.at[aux, rows_of(h)], swapped(m))
+
+    def turn(h):
+        for d in (0, 1, 3, 2):
+            t = (y + d) % 4
+            if d:
+                got(y_out[h][3 - d], by_y.at[h, t], y_at(d))
+
+            @pl.when(t == x)
+            def _():
+                copy = local(4 * h + 2, by_y.at[h, t], by_x.at[h, x])
+                copy.start()
+                copy.wait()
+
+            @pl.when(t != x)
+            def _():
+                along_x(h, d).start()
+
+    def swap(h):
+        for m in range(4):
+            @pl.when(m != x)
+            def _():
+                got(t_out[h][m], by_x.at[h, m], at(col_=2 * m + zlo))
+
+            here = jnp.logical_and(same_core, aux == m)
+
+            @pl.when(here)
+            def _():
+                copy = local(4 * h + 3, by_x.at[h, m], mirror.at[aux, rows_of(h)])
+                copy.start()
+                copy.wait()
+
+            @pl.when(jnp.logical_not(here))
+            def _():
+                along_z(h, m).start()
+
+    def arrive(h):
+        for d in (1, 2, 3):
+            got(x_out[h][d - 1], direct.at[(x + 4 - d) % 4, rows_of(h)], x_at(4 - d))
+        for r in range(4):
+            @pl.when(jnp.logical_not(jnp.logical_and(same_core, aux == r)))
+            def _():
+                got(m_out[h][r], mirror.at[r, rows_of(h)], swapped(r))
+
     for t in range(1, 5):
         for h in range(STEPS):
             reduce_step(h, t)
-
-    x_out = [[slot() for _ in range(3)] for _ in range(STEPS)]
-    m_out = [[slot() for _ in range(4)] for _ in range(STEPS)]
-    for h in range(STEPS):
-        rows = pl.ds(CH * h, CH)
-        mine = fock.at[h, aux, zlo]
-
-        def lanes_of(t):
-            return pl.ds(pl.multiple_of(128 * t, 128), PIECE)
-
-        for d in (1, 2, 3):
-            put(x_out[h][d - 1], mine.at[:, lanes_of((x + d) % 4)], direct.at[x, rows], x_at(d))
-        for t in range(4):
-            copy_args = (mine.at[:, lanes_of(t)], mirror.at[aux, rows])
-            here = jnp.logical_and(on_diagonal, y == t)
-
-            @pl.when(here)
-            def _():
-                local = pltpu.make_async_copy(*copy_args, loc.at[STEPS + h])
-                local.start()
-                local.wait()
-
-            @pl.when(jnp.logical_not(here))
-            def _():
-                pltpu.make_async_remote_copy(
-                    src_ref=copy_args[0], dst_ref=copy_args[1],
-                    send_sem=send.at[m_out[h][t]], recv_sem=recv.at[m_out[h][0] + aux],
-                    device_id=mirror_to(t), device_id_type=pl.DeviceIdType.MESH).start()
-        local = pltpu.make_async_copy(mine.at[:, lanes_of(x)], direct.at[x, rows], loc.at[h])
-        local.start()
-        local.wait()
-
-    for h in range(STEPS):
-        rows = pl.ds(CH * h, CH)
-        for d in (1, 2, 3):
-            got(x_out[h][d - 1], direct.at[(x + 4 - d) % 4, rows], x_at(4 - d))
-        for r in range(4):
-            @pl.when(jnp.logical_not(jnp.logical_and(on_diagonal, aux == r)))
-            def _():
-                got(m_out[h][r], mirror.at[r, rows], mirror_from(r))
-
+            if t == 4:
+                leave(h)
+                if h > 0:
+                    turn(h - 1)
+    turn(STEPS - 1)
+    for h in range(STEPS):
+        swap(h)
+    for h in range(STEPS):
+        arrive(h)
     for copy in sends:
         copy.wait_send()
     for h in range(STEPS):
-        rows = pl.ds(CH * h, CH)
-        for t in range(4):
-            @pl.when(jnp.logical_not(jnp.logical_and(on_diagonal, y == t)))
-            def _():
-                pltpu.make_async_remote_copy(
-                    src_ref=fock.at[h, aux, zlo, :, pl.ds(0, PIECE)], dst_ref=mirror.at[aux, rows],
-                    send_sem=send.at[m_out[h][t]], recv_sem=recv.at[m_out[h][0] + aux],
-                    device_id=mirror_to(t), device_id_type=pl.DeviceIdType.MESH).wait_send()
-
-
-COPIES = 3 + 4 * STEPS + 12 + 16 + 8 * STEPS + 7 * STEPS
+        for d in range(4):
+            @pl.when((y + d) % 4 != x)
+            def _():
+                along_x(h, d).wait_send()
+        for m in range(4):
+            @pl.when(jnp.logical_not(jnp.logical_and(same_core, aux == m)))
+            def _():
+                along_z(h, m).wait_send()
+
+
+COPIES = 3 + 4 * STEPS + 12 + 16 + 8 * STEPS + 14 * STEPS
 
 
 def exchange(slabs, gammas):
@@ -274,9 +318,11 @@
             pltpu.VMEM((STEPS, 4, 2, CH, WIDE), jnp.float32),
             pltpu.VMEM((2, STEPS, HALF, WIDE), jnp.float32),
             pltpu.VMEM((2, STEPS, 3, CH, WIDE), jnp.float32),
+            pltpu.VMEM((STEPS, 4, CH, PIECE), jnp.float32),
+            pltpu.VMEM((STEPS, 4, CH, PIECE), jnp.float32),
             pltpu.SemaphoreType.DMA((COPIES,)),
             pltpu.SemaphoreType.DMA((COPIES,)),
-            pltpu.SemaphoreType.DMA((2 * STEPS,)),
+            pltpu.SemaphoreType.DMA((4 * STEPS,)),
         ],
         compiler_params=pltpu.CompilerParams(
             collective_id=0, has_side_effects=True, vmem_limit_bytes=48 * 1024 * 1024),

time: 155 us -> 112 us (0.72); the launches traced: 152 us -> 111 us
  Pallas kernels: 142 us -> 102 us
    pallas_call x1, Pallas kernels: 142 us -> 102 us  [exchange(): pl.pallas_call(kernel, out_shape=(out, out), in_specs=[vmem, vmem], out_s...]
where the time goes in v2:
time: 112 us; the launch traced here: 111 us
  Pallas kernels  102 us (91%)
  local copies, waits for them, and re-layouts  6.63 us (6%)
  other arithmetic  1.91 us (2%)
    pallas_call x1, Pallas kernels, exchange(): pl.pallas_call(kernel, out_shape=(out, out), in_specs=[vmem, vmem], out_s...  102 us

profile of v2, /device:TPU:4, one launch (start us, length us, event | category | flops | bytes accessed | tf_op | source)
XLA Modules:
  0.0 110.8 jit_solution(3228678937527255496)
XLA Ops:
  0.7 1.3 %reshape.28 = bf16[4,158,512]{2,1,0:T(8,128)(2,1)S(1)} reshape(bf16[632,4,128]{2,1,0:T(4,128)(2,1)} %param.4) | data formatting | bytes 1294336 | tf_op jit(solution)/shard_map/reshape | solution.py:339
  2.0 0.1 pad.7
  2.0 0.0 copy-start
  2.1 1.0 copy-done
  3.1 0.2 reshape.31
  3.4 0.1 pad.8.g_ref
  3.4 101.5 %shard_map.59 = (f32[4,160,256]{2,1,0:T(8,128)S(1)}, f32[4,160,256]{2,1,0:T(8,128)S(1)}) custom-call(bf16[2,320,512]{2,1,0:T(8,128)(2,1)S(1)} %bitcast.14, bf16[4,160,512]{2,1,0:T(8,128)(2,1)S(1)} %pad.8.g_ref), custom_call_target="tpu_custom_call" | custom-call | flops 3355443200 | bytes 4194304 | tf_op jit(solution)/shard_map/pallas_call | solution.py:310
  105.0 0.2 constant_dynamic-slice_fusion
  105.2 0.1 reshape.34
  105.3 0.2 copy.9
  105.5 0.2 dynamic-slice_bitcast_fusion
  105.7 0.4 copy.7
  106.2 0.4 reshape.32
  106.6 0.8 broadcast_multiply_fusion
  107.3 0.8 dynamic_slice.22
  108.1 0.8 dynamic_slice.21
  108.9 0.8 dynamic_slice.23
  109.7 1.1 %add_divide_fusion = (f32[158,632]{1,0:T(8,128)}, f32[158,632]{1,0:T(8,128)}) fusion(f32[632]{0:T(1024)S(1)} %dynamic_slice.23, f32[158]{0:T(256)S(1)} %dynamic_slice.22, s32[158]{0:T(256)S(1)} %get-tuple-element.8, s32[632]{0:T(1024)S(1)} %dynamic_slice.21, s32[158]{0:T(256)S(1)} %get-tuple-element.9, f32[158,632]{1,0:T(8,128)S(1)} %reshape.32, ...), kind=kLoop, calls=%fused_computation.3 | loop fusion | flops 1298128 | bytes 1604648 | tf_op jit(solution)/shard_map/div | solution.py:357
  (1 shorter events, 0.0 us)
Async XLA Ops:
  2.0 1.1 copy-start

commit v3 on v2

--- a/solution.py
+++ b/solution.py
@@ -10,13 +10,32 @@
 SUB = 160
 STEPS = 2
 CH = SUB // STEPS
-HALF = CH // 2
+LAST = CH - 1
 WIDE = 4 * SUB
 KX = 512
 PIECE = 256
-
-
-def kernel(s_ref, g_ref, direct, mirror, sbuf, gbuf, fock, rs_half, rs_full, by_y, by_x, send, recv, loc):
+TOP = 32760.0
+FINE = 128.0
+
+
+def encode(v):
+    inside = lax.broadcasted_iota(jnp.int32, v.shape, 0) < LAST
+    size = jnp.where(inside, jnp.abs(v), 0.0)
+    largest = jnp.maximum(jnp.max(size, axis=0, keepdims=True), 1e-30)
+    scale = jnp.ceil(jnp.log2(largest) * FINE)
+    code = (jnp.sqrt(size) * (jnp.exp2(scale * (-0.5 / FINE)) * TOP) + 0.5).astype(jnp.int32)
+    code = jnp.where(v < 0.0, -code, code)
+    return jnp.where(inside, code, scale.astype(jnp.int32)).astype(jnp.int16)
+
+
+def decode(code):
+    value = code.astype(jnp.int32).astype(jnp.float32)
+    root = value * (jnp.exp2(value[LAST:CH] * (0.5 / FINE)) * (1.0 / TOP))
+    return root * jnp.abs(root)
+
+
+def kernel(s_ref, g_ref, direct, mirror, sbuf, gbuf, fock, out_codes, in_codes, reduced, direct_codes, mirror_codes,
+           by_y, by_x, send, recv, loc):
     row, col, aux = lax.axis_index("row"), lax.axis_index("col"), lax.axis_index("aux")
     y, c = row // 2, row % 2
     x, zlo = col // 2, col % 2
@@ -137,14 +156,17 @@
 
     spread(0)
     for h in range(STEPS):
-        send_rows(h)
         sbuf[h, :, 0:KX] = s_ref[h]
     for d in (1, 3, 2):
         p = (4 - d) % 4
         got(a2a[d], piece(c, y, p), x_at(4 - d))
         spread(p)
+        if d == 3:
+            send_rows(0)
     relay(0)
     relay(3)
+    for h in range(1, STEPS):
+        send_rows(h)
     relay(1)
     forward_rows(0)
     relay(2)
@@ -154,7 +176,7 @@
         for p in range(4):
             got(cross[d][p], piece(1 - c, (y + d) % 4, p), other)
 
-    rs_send = [[[slot() for _ in range(4)] for _ in range(2)] for _ in range(STEPS)]
+    rs = [[[slot() for _ in range(4 - (h + way) % 2)] for way in range(2)] for h in range(STEPS)]
 
     def multiply(h):
         def column_block(cc, carry):
@@ -170,39 +192,54 @@
         there = (z + d) % 8
         return h, there // 2, there % 2
 
-    halves = (pl.ds(0, HALF), pl.ds(HALF, HALF))
-
-    def reduce_step(h, t):
+    def tiles(body):
+        def one(i, carry):
+            body(pl.ds(pl.multiple_of(128 * i, 128), 128))
+            return carry
+
+        lax.fori_loop(0, WIDE // 128, one, 0)
+
+    def reduce_step(h, way, step):
+        hops = len(rs[h][way])
+        sign = 1 if way == 0 else 7
+        here = chunk(h, sign * (hops - step))
+        if step > 0:
+            got(rs[h][way][step - 1], in_codes.at[h, way, step - 1], z_at(8 - sign))
+
+        def one(cols):
+            v = fock[(*here, slice(None), cols)]
+            if step > 0:
+                v += decode(in_codes[h, way, step - 1, :, cols])
+            out_codes[h, way, step, :, cols] = encode(v)
+
+        tiles(one)
+        put(rs[h][way][step], out_codes.at[h, way, step], in_codes.at[h, way, step], z_at(sign))
+
+    def reduce_last(h):
         for way in range(2):
-            sign = 1 if way == 0 else 7
-            nxt, prev = z_at(sign), z_at(8 - sign)
-            here = chunk(h, sign * (4 - t))
-            if t == 0:
-                put(rs_send[h][way][0], fock.at[(*here, halves[way])], rs_half.at[way, h], nxt)
-                continue
-            if t == 1:
-                got(rs_send[h][way][0], rs_half.at[way, h], prev)
-                fock[(*here, halves[way])] += rs_half[way, h]
-            else:
-                got(rs_send[h][way][t - 1], rs_full.at[way, h, t - 2], prev)
-                fock[here] += rs_full[way, h, t - 2]
-            if t < 4:
-                put(rs_send[h][way][t], fock.at[here], rs_full.at[way, h, t - 1], nxt)
+            got(rs[h][way][-1], in_codes.at[h, way, len(rs[h][way]) - 1], z_at(7 if way == 0 else 1))
+
+        def one(cols):
+            v = fock[(*chunk(h, 0), slice(None), cols)]
+            for way in range(2):
+                v += decode(in_codes[h, way, len(rs[h][way]) - 1, :, cols])
+            reduced[h, :, cols] = encode(v)
+
+        tiles(one)
 
     for h in range(STEPS):
         if h > 0:
             forward_rows(h)
         finish_rows(h)
         multiply(h)
-        reduce_step(h, 0)
+        for way in range(2):
+            reduce_step(h, way, 0)
+
     x_out = [[slot() for _ in range(3)] for _ in range(STEPS)]
     y_out = [[slot() for _ in range(3)] for _ in range(STEPS)]
     t_out = [[slot() for _ in range(4)] for _ in range(STEPS)]
     m_out = [[slot() for _ in range(4)] for _ in range(STEPS)]
 
-    def rows_of(h):
-        return pl.ds(CH * h, CH)
-
     def lanes_of(t):
         return pl.ds(pl.multiple_of(128 * t, 128), PIECE)
 
@@ -215,13 +252,13 @@
             device_id=dev, device_id_type=pl.DeviceIdType.MESH)
 
     def leave(h):
-        mine = fock.at[h, aux, zlo]
+        mine = reduced.at[h]
         for d in (2, 1, 3):
             put(y_out[h][d - 1], mine.at[:, lanes_of((y + d) % 4)], by_y.at[h, y], y_at(d))
         for d in (2, 1, 3):
-            put(x_out[h][d - 1], mine.at[:, lanes_of((x + d) % 4)], direct.at[x, rows_of(h)], x_at(d))
+            put(x_out[h][d - 1], mine.at[:, lanes_of((x + d) % 4)], direct_codes.at[x, h], x_at(d))
         copies = (local(4 * h, mine.at[:, lanes_of(y)], by_y.at[h, y]),
-                  local(4 * h + 1, mine.at[:, lanes_of(x)], direct.at[x, rows_of(h)]))
+                  local(4 * h + 1, mine.at[:, lanes_of(x)], direct_codes.at[x, h]))
         for copy in copies:
             copy.start()
         for copy in copies:
@@ -232,7 +269,7 @@
         return remote(t_out[h][d], t_out[h][0] + x, by_y.at[h, t], by_x.at[h, x], at(col_=2 * t + zlo))
 
     def along_z(h, m):
-        return remote(m_out[h][m], m_out[h][0] + aux, by_x.at[h, m], mirror.at[aux, rows_of(h)], swapped(m))
+        return remote(m_out[h][m], m_out[h][0] + aux, by_x.at[h, m], mirror_codes.at[aux, h], swapped(m))
 
     def turn(h):
         for d in (0, 1, 3, 2):
@@ -260,7 +297,7 @@
 
             @pl.when(here)
             def _():
-                copy = local(4 * h + 3, by_x.at[h, m], mirror.at[aux, rows_of(h)])
+                copy = local(4 * h + 3, by_x.at[h, m], mirror_codes.at[aux, h])
                 copy.start()
                 copy.wait()
 
@@ -270,24 +307,35 @@
 
     def arrive(h):
         for d in (1, 2, 3):
-            got(x_out[h][d - 1], direct.at[(x + 4 - d) % 4, rows_of(h)], x_at(4 - d))
+            got(x_out[h][d - 1], direct_codes.at[(x + 4 - d) % 4, h], x_at(4 - d))
         for r in range(4):
             @pl.when(jnp.logical_not(jnp.logical_and(same_core, aux == r)))
             def _():
-                got(m_out[h][r], mirror.at[r, rows_of(h)], swapped(r))
-
-    for t in range(1, 5):
+                got(m_out[h][r], mirror_codes.at[r, h], swapped(r))
+
+    for step in range(1, 5):
         for h in range(STEPS):
-            reduce_step(h, t)
-            if t == 4:
-                leave(h)
-                if h > 0:
-                    turn(h - 1)
+            for way in range(2):
+                if step < len(rs[h][way]):
+                    reduce_step(h, way, step)
+    for h in range(STEPS):
+        reduce_last(h)
+        leave(h)
+        if h > 0:
+            turn(h - 1)
     turn(STEPS - 1)
     for h in range(STEPS):
         swap(h)
     for h in range(STEPS):
         arrive(h)
+
+    def unpack(i, carry):
+        for h in range(STEPS):
+            direct[i, h] = pltpu.roll(decode(direct_codes[i, h]), (PIECE - 32 * x) % PIECE, 1)
+            mirror[i, h] = pltpu.roll(decode(mirror_codes[i, h]), (PIECE - 32 * y) % PIECE, 1)
+        return carry
+
+    lax.fori_loop(0, 4, unpack, 0)
     for copy in sends:
         copy.wait_send()
     for h in range(STEPS):
@@ -301,12 +349,12 @@
                 along_z(h, m).wait_send()
 
 
-COPIES = 3 + 4 * STEPS + 12 + 16 + 8 * STEPS + 14 * STEPS
+COPIES = 3 + 4 * STEPS + 12 + 16 + 7 * STEPS + 14 * STEPS
 
 
 def exchange(slabs, gammas):
     vmem = pl.BlockSpec(memory_space=pltpu.VMEM)
-    out = jax.ShapeDtypeStruct((4, SUB, PIECE), jnp.float32)
+    out = jax.ShapeDtypeStruct((4, STEPS, CH, PIECE), jnp.float32)
     return pl.pallas_call(
         kernel,
         out_shape=(out, out),
@@ -316,10 +364,13 @@
             pltpu.VMEM((STEPS, 4 * CH, 4 * KX), jnp.bfloat16),
             pltpu.VMEM((2, 4, SUB, 4 * KX), jnp.bfloat16),
             pltpu.VMEM((STEPS, 4, 2, CH, WIDE), jnp.float32),
-            pltpu.VMEM((2, STEPS, HALF, WIDE), jnp.float32),
-            pltpu.VMEM((2, STEPS, 3, CH, WIDE), jnp.float32),
-            pltpu.VMEM((STEPS, 4, CH, PIECE), jnp.float32),
-            pltpu.VMEM((STEPS, 4, CH, PIECE), jnp.float32),
+            pltpu.VMEM((STEPS, 2, 4, CH, WIDE), jnp.int16),
+            pltpu.VMEM((STEPS, 2, 4, CH, WIDE), jnp.int16),
+            pltpu.VMEM((STEPS, CH, WIDE), jnp.int16),
+            pltpu.VMEM((4, STEPS, CH, PIECE), jnp.int16),
+            pltpu.VMEM((4, STEPS, CH, PIECE), jnp.int16),
+            pltpu.VMEM((STEPS, 4, CH, PIECE), jnp.int16),
+            pltpu.VMEM((STEPS, 4, CH, PIECE), jnp.int16),
             pltpu.SemaphoreType.DMA((COPIES,)),
             pltpu.SemaphoreType.DMA((COPIES,)),
             pltpu.SemaphoreType.DMA((4 * STEPS,)),
@@ -335,16 +386,13 @@
     block = slabs.shape[0]
     sub = block // 4
 
-    def pieces(a):
-        return jnp.pad(a.reshape(4, sub, KX), ((0, 0), (0, SUB - sub), (0, 0)))
-
     row, col, aux = lax.axis_index("row"), lax.axis_index("col"), lax.axis_index("aux")
-    s = pieces(slabs).reshape(4, STEPS, CH, KX).transpose(1, 0, 2, 3).reshape(STEPS, 4 * CH, KX)
-    direct, mirror = exchange(s, pieces(gammas))
-    own = lax.dynamic_slice_in_dim(direct[:, :sub], 32 * (col // 2), sub, axis=2)
-    other = lax.dynamic_slice_in_dim(mirror[:, :sub], 32 * (row // 2), sub, axis=2)
-    own = own.transpose(1, 0, 2).reshape(sub, block)
-    other = other.reshape(block, sub).T
+    s = slabs.reshape(4, STEPS, sub // STEPS, KX).transpose(1, 0, 2, 3)
+    s = jnp.pad(s, ((0, 0), (0, 0), (0, CH - sub // STEPS), (0, 0))).reshape(STEPS, 4 * CH, KX)
+    g = jnp.pad(gammas.reshape(4, sub, KX), ((0, 0), (0, SUB - sub), (0, 0)))
+    direct, mirror = exchange(s, g)
+    own = direct[:, :, :LAST, :sub].transpose(1, 2, 0, 3).reshape(sub, block)
+    other = mirror[:, :, :LAST, :sub].reshape(block, sub).T
     gradient = 2.0 * (own - other)
     row_start = row * block + aux * sub
     col_start = col * block

time: 112 us -> 90.6 us (0.81)
  Pallas kernels: 102 us -> 80.2 us
    pallas_call x1, Pallas kernels: 102 us -> 80.2 us  [exchange(): pl.pallas_call(kernel, out_shape=(out, out), in_specs=[vmem, vmem], out_s...]
where the time goes in v3:
time: 90.6 us; the launch traced here: 89.3 us
  Pallas kernels  80.2 us (89%)
  local copies, waits for them, and re-layouts  6.44 us (7%)
  other arithmetic  1.92 us (2%)
    pallas_call x1, Pallas kernels, exchange(): pl.pallas_call(kernel, out_shape=(out, out), in_specs=[vmem, vmem], out_s...  80.2 us

profile of v3, /device:TPU:4, one launch (start us, length us, event | category | flops | bytes accessed | tf_op | source)
XLA Modules:
  0.0 89.3 jit_solution(174724661241459275)
XLA Ops:
  0.6 0.8 dynamic_slice.14
  1.4 0.8 broadcast_multiply_fusion
  2.2 0.8 dynamic_slice.13
  3.0 0.8 dynamic_slice.15
  3.7 1.6 %reshape.25 = bf16[4,2,79,512]{3,2,1,0:T(8,128)(2,1)S(1)} reshape(bf16[632,4,128]{2,1,0:T(4,128)(2,1)} %param.4) | data formatting | bytes 1294336 | tf_op jit(solution)/shard_map/reshape | solution.py:390
  5.4 0.0 copy-start
  5.4 0.1 pad.8.clone
  5.4 1.0 %copy-done = bf16[632,4,128]{2,1,0:T(4,128)(2,1)S(1)} copy-done((bf16[632,4,128]{2,1,0:T(4,128)(2,1)S(1)}, bf16[632,4,128]{2,1,0:T(4,128)(2,1)}, u32[]{:S(2)}) %copy-start) | copy-done | bytes 647192
  6.4 0.2 reshape.27
  6.7 0.1 pad.9.g_ref
  6.8 80.2 %shard_map.59 = (f32[4,2,80,256]{3,2,1,0:T(8,128)S(1)}, f32[4,2,80,256]{3,2,1,0:T(8,128)S(1)}) custom-call(bf16[2,320,512]{2,1,0:T(8,128)(2,1)S(1)} %bitcast.11, bf16[4,160,512]{2,1,0:T(8,128)(2,1)S(1)} %pad.9.g_ref), custom_call_target="tpu_custom_call" | custom-call | flops 3355443200 | bytes 4194304 | tf_op jit(solution)/shard_map/pallas_call | solution.py:358
  87.0 0.4 copy.9
  87.4 0.4 reshape.28
  87.8 0.1 reshape.30
  87.9 0.2 copy.11
  88.1 1.2 %add_divide_fusion = (f32[158,632]{1,0:T(8,128)}, f32[158,632]{1,0:T(8,128)}) fusion(f32[632]{0:T(1024)S(1)} %dynamic_slice.15, f32[158]{0:T(256)S(1)} %dynamic_slice.14, s32[158]{0:T(256)S(1)} %get-tuple-element.8, s32[632]{0:T(1024)S(1)} %dynamic_slice.13, s32[158]{0:T(256)S(1)} %get-tuple-element.9, f32[158,632]{1,0:T(8,128)S(1)} %reshape.28, ...), kind=kLoop, calls=%fused_computation.3 | loop fusion | flops 1298128 | bytes 1604648 | tf_op jit(solution)/shard_map/div | solution.py:405
  (2 shorter events, 0.1 us)
Async XLA Ops:
  5.4 1.1 %copy-start = (bf16[632,4,128]{2,1,0:T(4,128)(2,1)S(1)}, bf16[632,4,128]{2,1,0:T(4,128)(2,1)}, u32[]{:S(2)}) copy-start(bf16[632,4,128]{2,1,0:T(4,128)(2,1)} %param.5) | copy-start | bytes 1941508

commit v4 on v0

v4 whole, which is shorter than its diff:
```python
import jax
import jax.numpy as jnp
from jax import lax
from jax.experimental import pallas as pl
from jax.experimental.pallas import tpu as pltpu
from jax.sharding import PartitionSpec as P

SUB = 160
ROWS = (96, 64)
FIRST = (0, ROWS[0])
LANES = 128
REST = SUB - LANES
WIDE = 4 * SUB
KX = 512
FOLD = tuple(-(-r // 32) * 8 for r in ROWS)
PACKED = tuple(r + -(-f // 16) * 16 for r, f in zip(ROWS, FOLD))
TOP = 32760.0
FINE = 128.0
PLACE = (0, 1, 3, 2)
GROUPS = ((0, 0, 3 * LANES, 1), (0, 3 * LANES, WIDE, 1), (1, 0, WIDE, 0))
MESH = pl.DeviceIdType.MESH


def encode(v):
    last = v.shape[0] - 1
    inside = lax.broadcasted_iota(jnp.int32, v.shape, 0) < last
    size = jnp.where(inside, jnp.abs(v), 0.0)
    largest = jnp.maximum(jnp.max(size, axis=0, keepdims=True), 1e-30)
    scale = jnp.ceil(jnp.log2(largest) * FINE)
    code = (jnp.sqrt(size) * (jnp.exp2(scale * (-0.5 / FINE)) * TOP) + 0.5).astype(jnp.int32)
    code = jnp.where(v < 0.0, -code, code)
    return jnp.where(inside, code, scale.astype(jnp.int32)).astype(jnp.int16)


def decode(code):
    value = code.astype(jnp.int32).astype(jnp.float32)
    root = value * (jnp.exp2(value[value.shape[0] - 1:] * (0.5 / FINE)) * (1.0 / TOP))
    return root * jnp.abs(root)


def fold(rest, t, h):
    size = FOLD[h]
    lane = lax.broadcasted_iota(jnp.int32, (size, LANES), 1)
    out = jnp.zeros((size, LANES), jnp.int32)
    for g in range(4):
        rows = rest[size * g:min(size * (g + 1), ROWS[h])]
        if rows.shape[0] < size:
            rows = jnp.concatenate([rows, jnp.zeros((size - rows.shape[0], LANES), jnp.int32)], axis=0)
        if g != t:
            rows = pltpu.roll(rows, (REST * (g - t)) % LANES, 1)
        out = jnp.where(lane // REST == g, rows, out)
    more = PACKED[h] - ROWS[h] - size
    return jnp.concatenate([out, jnp.zeros((more, LANES), jnp.int32)], axis=0) if more else out


def unfold(codes, h):
    parts = []
    for g in range(4):
        rows = codes[:min(FOLD[h], ROWS[h] - FOLD[h] * g)]
        parts.append(pltpu.roll(rows, LANES - REST * g, 1) if g else rows)
    return jnp.concatenate(parts, axis=0)


def kernel(s_ref, g_ref, direct, mirror, sbuf, gbuf, fock, *rest):
    n = len(GROUPS)
    outgoing, incoming, rest = rest[:n], rest[n:2 * n], rest[2 * n:]
    reduced, packed, direct_codes, mirror_codes, by_y, by_x = (rest[2 * i:2 * i + 2] for i in range(6))
    send, recv, loc = rest[12:]

    row, col, aux = lax.axis_index("row"), lax.axis_index("col"), lax.axis_index("aux")
    y, c = row // 2, row % 2
    x, zlo = col // 2, col % 2
    z = 2 * aux + zlo

    def at(row_=row, col_=col, aux_=aux):
        return {"row": row_, "col": col_, "aux": aux_}

    def x_at(d):
        return at(col_=2 * ((x + d) % 4) + zlo)

    def y_at(d):
        return at(row_=2 * ((y + d) % 4) + c)

    def z_at(d):
        there = (z + d) % 8
        return at(col_=2 * x + there % 2, aux_=there // 2)

    def swapped(m):
        return at(2 * y + zlo, 2 * x + c, m)

    other = at(row_=2 * y + (1 - c))
    same_core = zlo == c

    barrier = pltpu.get_barrier_semaphore()

    def greet(dev):
        pl.semaphore_signal(barrier, inc=1, device_id=dev, device_id_type=MESH)

    for dev in (x_at(1), x_at(3), x_at(2), y_at(1), y_at(3), y_at(2), other, z_at(1), z_at(7)):
        greet(dev)
    for r in range(4):
        @pl.when(jnp.logical_not(jnp.logical_and(same_core, aux == r)))
        def _():
            greet(swapped(r))

    pl.semaphore_wait(barrier, 13 - same_core.astype(jnp.int32))

    sends = []
    count = [0]

    def slots(k):
        count[0] += k
        return list(range(count[0] - k, count[0]))

    def remote(n_send, n_recv, src, dst, dev):
        return pltpu.make_async_remote_copy(
            src_ref=src, dst_ref=dst, send_sem=send.at[n_send], recv_sem=recv.at[n_recv],
            device_id=dev, device_id_type=MESH)

    def put(n, src, dst, dev):
        copy = remote(n, n, src, dst, dev)
        copy.start()
        sends.append(copy)

    def got(n, dst, dev):
        remote(n, n, dst, dst, dev).wait_recv()

    lanes = [pl.ds(KX * p, KX) for p in range(4)]

    a2a, cross = slots(4), [slots(4) for _ in range(4)]
    g_out = [slots(4) for _ in range(4)]

    def piece(core, d, p):
        return gbuf.at[core, PLACE[d % 4], :, lanes[p]]

    def over(d, p):
        put(cross[d][p], piece(c, d, p), piece(c, d, p), other)

    def spread(p):
        for d in (1, 3):
            put(g_out[p][d], piece(c, 0, p), piece(c, 4 - d, p), y_at(d))
        over(0, p)

    def arrived(d):
        p = (4 - d) % 4
        got(a2a[d], piece(c, 0, p), x_at(4 - d))
        spread(p)

    def relay(p):
        for d in (3, 1):
            here = piece(c, d, p)
            got(g_out[p][4 - d], here, y_at(d))
            if d == (3 if p in (0, 1) else 1):
                put(g_out[p][2], here, piece(c, 2, p), y_at(4 - d))
            over(d, p)

    def relay_far(p):
        got(g_out[p][2], piece(c, 2, p), y_at(3 if p in (0, 1) else 1))
        over(2, p)

    def crossed(d):
        for p in range(4):
            got(cross[d][p], piece(1 - c, d, p), other)

    s_out = [slots(5) for _ in ROWS]

    def chunk_rows(h):
        return pl.ds(4 * FIRST[h], 4 * ROWS[h])

    def half_rows(h, i):
        return pl.ds(4 * FIRST[h] + 2 * ROWS[h] * i, 2 * ROWS[h])

    def send_rows(h):
        for d in (1, 3):
            put(s_out[h][d], s_ref.at[chunk_rows(h)], sbuf.at[chunk_rows(h), lanes[4 - d]], x_at(d))

    def forward_rows(h):
        for i, d in enumerate((1, 3)):
            got(s_out[h][d], sbuf.at[chunk_rows(h), lanes[4 - d]], x_at(4 - d))
            put(s_out[h][2 * i + 2], sbuf.at[half_rows(h, i), lanes[4 - d]],
                sbuf.at[half_rows(h, i), lanes[2]], x_at(d))

    def finish_rows(h):
        for i, d in enumerate((1, 3)):
            got(s_out[h][2 * i + 2], sbuf.at[half_rows(h, i), lanes[2]], x_at(4 - d))

    def multiply(h, core, near, far):
        a = sbuf[4 * FIRST[h]:4 * (FIRST[h] + ROWS[h])]

        def block(b, first, size):
            out = lax.dot_general(a, b, (((1,), (1,)), ((), ())), preferred_element_type=jnp.float32)
            fock[:, core, FIRST[h]:FIRST[h] + ROWS[h], first:first + size] = out.reshape(4, ROWS[h], size)

        if near and far:
            block(gbuf[core, :, 0:LANES].reshape(4 * LANES, 4 * KX), 0, 4 * LANES)
        elif near:
            block(gbuf[core, 0:3, 0:LANES].reshape(3 * LANES, 4 * KX), 0, 3 * LANES)
        elif far:
            block(gbuf[core, 3, 0:LANES], 3 * LANES, LANES)
        if far:
            block(gbuf[core, :, LANES:SUB].reshape(4 * REST, 4 * KX), 4 * LANES, 4 * REST)

    rs = [[slots(4 if way == longer else 3) for way in range(2)] for _, _, _, longer in GROUPS]

    def sums(k, d, i):
        h, first, _, _ = GROUPS[k]
        there = (z + d) % 8
        return there // 2, there % 2, pl.ds(FIRST[h], ROWS[h]), pl.ds(first + LANES * i, LANES)

    def tiles(k):
        return range((GROUPS[k][2] - GROUPS[k][1]) // LANES)

    def hop(k, step):
        for way in range(2):
            hops = len(rs[k][way])
            if step >= hops:
                continue
            sign = 1 if way == 0 else 7
            if step > 0:
                got(rs[k][way][step - 1], incoming[k].at[way, step - 1], z_at(8 - sign))
            for i in tiles(k):
                cols = pl.ds(LANES * i, LANES)
                v = fock[sums(k, sign * (hops - step), i)]
                if step > 0:
                    v += decode(incoming[k][way, step - 1, :, cols])
                outgoing[k][way, step, :, cols] = encode(v)
            put(rs[k][way][step], outgoing[k].at[way, step], incoming[k].at[way, step], z_at(sign))

    def own(k):
        h, first, _, _ = GROUPS[k]
        for way in range(2):
            hops = len(rs[k][way])
            got(rs[k][way][-1], incoming[k].at[way, hops - 1], z_at(7 if way == 0 else 1))
        for i in tiles(k):
            v = fock[sums(k, 0, i)]
            for way in range(2):
                v += decode(incoming[k][way, len(rs[k][way]) - 1, :, pl.ds(LANES * i, LANES)])
            reduced[h][:, first + LANES * i:first + LANES * (i + 1)] = encode(v)

    x_out, y_out = [slots(4) for _ in ROWS], [slots(4) for _ in ROWS]
    t_out, m_out = [slots(4) for _ in ROWS], [slots(4) for _ in ROWS]

    def local(n, src, dst):
        return pltpu.make_async_copy(src, dst, loc.at[n])

    def leave(h):
        shared = reduced[h][:, 4 * LANES:].astype(jnp.int32)
        for d in (2, 1, 3, 0):
            t = PLACE[d]
            packed[h][d, 0:ROWS[h]] = reduced[h][:, LANES * t:LANES * (t + 1)]
            packed[h][d, ROWS[h]:PACKED[h]] = fold(shared, t, h).astype(jnp.int16)
            if d:
                put(y_out[h][d], packed[h].at[d], by_y[h].at[y], y_at(d))
        for d in (2, 1, 3):
            put(x_out[h][d], packed[h].at[(x + d - y + 4) % 4], direct_codes[h].at[x], x_at(d))
        copies = (local(4 * h, packed[h].at[0], by_y[h].at[y]),
                  local(4 * h + 1, packed[h].at[(x - y + 4) % 4], direct_codes[h].at[x]))
        for copy in copies:
            copy.start()
        for copy in copies:
            copy.wait()

    def along_x(h, d):
        t = (y + d) % 4
        return remote(t_out[h][d], t_out[h][0] + x, by_y[h].at[t], by_x[h].at[x], at(col_=2 * t + zlo))

    def along_z(h, m):
        return remote(m_out[h][m], m_out[h][0] + aux, by_x[h].at[m], mirror_codes[h].at[aux], swapped(m))

    def turn(h):
        for d in (0, 1, 3, 2):
            t = (y + d) % 4
            if d:
                got(y_out[h][4 - d], by_y[h].at[t], y_at(d))

            @pl.when(t == x)
            def _():
                copy = local(4 * h + 2, by_y[h].at[t], by_x[h].at[x])
                copy.start()
                copy.wait()

            @pl.when(t != x)
            def _():
                along_x(h, d).start()

    def swap(h):
        for m in range(4):
            @pl.when(m != x)
            def _():
                got(t_out[h][m], by_x[h].at[m], at(col_=2 * m + zlo))

            here = jnp.logical_and(same_core, aux == m)

            @pl.when(here)
            def _():
                copy = local(4 * h + 3, by_x[h].at[m], mirror_codes[h].at[aux])
                copy.start()
                copy.wait()

            @pl.when(jnp.logical_not(here))
            def _():
                along_z(h, m).start()

    def arrive(h):
        for d in (1, 2, 3):
            got(x_out[h][d], direct_codes[h].at[(x + 4 - d) % 4], x_at(4 - d))
        for r in range(4):
            @pl.when(jnp.logical_not(jnp.logical_and(same_core, aux == r)))
            def _():
                got(m_out[h][r], mirror_codes[h].at[r], swapped(r))

    def unpack(h):
        def one(i, carry):
            for codes, out in ((direct_codes[h], direct), (mirror_codes[h], mirror)):
                main, shared = codes[i, 0:ROWS[h]], codes[i, ROWS[h]:PACKED[h]].astype(jnp.int32)
                rows = slice(FIRST[h], FIRST[h] + ROWS[h])
                out[i, rows, 0:LANES] = decode(main)
                out[i, rows, LANES:2 * LANES] = decode(unfold(shared, h))
            return carry

        lax.fori_loop(0, 4, one, 0)

    for d in (1, 3, 2):
        put(a2a[d], g_ref.at[(x + d) % 4], piece(c, 0, 4 - d), x_at(d))
    gbuf[c, 0, :, 0:KX] = g_ref[x]
    spread(0)
    sbuf[:, 0:KX] = s_ref[...]
    arrived(1)
    arrived(3)
    send_rows(0)
    relay(0)
    arrived(2)
    relay(3)
    relay(1)
    forward_rows(0)
    send_rows(1)
    relay(2)
    for d in (0, 1, 3):
        crossed(d)
    finish_rows(0)
    multiply(0, c, True, False)
    multiply(0, 1 - c, True, False)
    hop(0, 0)
    for p in (0, 3, 1, 2):
        relay_far(p)
    multiply(0, c, False, True)
    forward_rows(1)
    hop(0, 1)
    crossed(2)
    multiply(0, 1 - c, False, True)
    hop(1, 0)
    hop(0, 2)
    finish_rows(1)
    multiply(1, c, True, True)
    multiply(1, 1 - c, True, True)
    hop(2, 0)
    hop(1, 1)
    hop(0, 3)
    hop(2, 1)
    hop(1, 2)
    own(0)
    hop(2, 2)
    hop(1, 3)
    own(1)
    leave(0)
    hop(2, 3)
    turn(0)
    own(2)
    leave(1)
    swap(0)
    turn(1)
    swap(1)
    arrive(0)
    unpack(0)
    arrive(1)
    unpack(1)
    for copy in sends:
        copy.wait_send()
    for h in range(2):
        for d in range(4):
            @pl.when((y + d) % 4 != x)
            def _():
                along_x(h, d).wait_send()
        for m in range(4):
            @pl.when(jnp.logical_not(jnp.logical_and(same_core, aux == m)))
            def _():
                along_z(h, m).wait_send()


COPIES = 4 + 16 + 16 + 10 + 7 * len(GROUPS) + 32


def exchange(slabs, gammas):
    vmem = pl.BlockSpec(memory_space=pltpu.VMEM)
    out = jax.ShapeDtypeStruct((4, SUB, 2 * LANES), jnp.float32)
    hops = [pltpu.VMEM((2, 4, ROWS[h], last - first), jnp.int16) for h, first, last, _ in GROUPS]
    pieces = [pltpu.VMEM((4, p, LANES), jnp.int16) for p in PACKED]
    return pl.pallas_call(
        kernel,
        out_shape=(out, out),
        in_specs=[vmem, vmem],
        out_specs=(vmem, vmem),
        scratch_shapes=[
            pltpu.VMEM((4 * SUB, 4 * KX), jnp.bfloat16),
            pltpu.VMEM((2, 4, SUB, 4 * KX), jnp.bfloat16),
            pltpu.VMEM((4, 2, SUB, WIDE), jnp.float32),
            *hops, *hops,
            *[pltpu.VMEM((r, WIDE), jnp.int16) for r in ROWS],
            *pieces, *pieces, *pieces, *pieces, *pieces,
            pltpu.SemaphoreType.DMA((COPIES,)),
            pltpu.SemaphoreType.DMA((COPIES,)),
            pltpu.SemaphoreType.DMA((8,)),
        ],
        compiler_params=pltpu.CompilerParams(
            collective_id=0, has_side_effects=True, vmem_limit_bytes=48 * 1024 * 1024),
        cost_estimate=pl.CostEstimate(
            flops=2 * 640 * 1280 * 2048, bytes_accessed=4 * 1024 * 1024, transcendentals=0),
    )(slabs, gammas)


def on_device(slabs, gammas, occupied, energies):
    block = slabs.shape[0]
    sub = block // 4
    row, col, aux = lax.axis_index("row"), lax.axis_index("col"), lax.axis_index("aux")
    split = ROWS[0] - 1
    rows = slabs.reshape(4, sub, KX)
    parts = [jnp.pad(part, ((0, 0), (0, 1), (0, 0))).reshape(-1, KX) for part in (rows[:, :split], rows[:, split:])]
    g = jnp.pad(gammas.reshape(4, sub, KX), ((0, 0), (0, SUB - sub), (0, 0)))
    direct, mirror = exchange(jnp.concatenate(parts), g)

    def trim(a):
        return jnp.concatenate([a[:, :split, :sub], a[:, split + 1:SUB - 1, :sub]], axis=1)

    own = trim(direct).transpose(1, 0, 2).reshape(sub, block)
    other = trim(mirror).reshape(block, sub).T
    gradient = 2.0 * (own - other)
    row_start = row * block + aux * sub
    col_start = col * block
    energy_rows = lax.dynamic_slice_in_dim(energies, row_start, sub)
    energy_cols = lax.dynamic_slice_in_dim(energies, col_start, block)
    occ_rows = lax.dynamic_slice_in_dim(occupied, row_start, sub)
    occ_cols = lax.dynamic_slice_in_dim(occupied, col_start, block)
    nonredundant = occ_rows[:, None] + occ_cols[None, :] - 2 * occ_rows[:, None] * occ_cols[None, :]
    denominator = 4.0 * jnp.abs(energy_rows[:, None] - energy_cols[None, :]) + 0.5
    rotation_step = -nonredundant.astype(jnp.float32) * gradient / denominator
    return (gradient, rotation_step)


def solution(mesh):
    placed = (P("row", "col", "aux"), P("row", "col", "aux"), P(), P())
    return jax.shard_map(
        on_device,
        mesh=mesh,
        in_specs=placed,
        out_specs=(P(("row", "aux"), "col"), P(("row", "aux"), "col")),
        check_vma=False,
    )
```

time: 654 us -> 86.9 us (0.13)
  blocking collectives: 417 us -> 0 us
  waiting for transfers between devices: 149 us -> 0 us
  Pallas kernels: 0 us -> 77.3 us
  local copies, waits for them, and re-layouts: 49.7 us -> 6.25 us
  between operations: 14.7 us -> 0.78 us
  matrix products: 10.9 us -> 0 us
    unnamed x1 -> x0, blocking collectives: 295 us -> none
    all_to_all x1 -> x0, blocking collectives: 122 us -> none  [on_device(): lax.all_to_all(reduced, ('row', 'aux'), split_axis=1, concat_axis=0, tile...]
    unnamed x4 -> x0, waiting for transfers between devices: 107 us -> none
    pallas_call x0 -> x1, Pallas kernels: none -> 77.3 us  [exchange(): pl.pallas_call(kernel, out_shape=(out, out), in_specs=[vmem, vmem], out_s...]
    all_gather x1 -> x0, waiting for transfers between devices: 42.3 us -> none  [on_device(): piece = lax.all_gather(gammas, 'row', axis=0, tiled=True)]
    all_to_all x4 -> x0, local copies, waits for them, and re-layouts: 26.8 us -> none  [on_device(): lax.all_to_all(reduced, ('row', 'aux'), split_axis=1, concat_axis=0, tile...]
    unnamed x11 -> x4, local copies, waits for them, and re-layouts: 20.5 us -> 1.03 us
    dot_general x1 -> x0, matrix products: 10.9 us -> none  [on_device(): jnp.dot(flat_slabs, flat_piece.T, preferred_element_type=jnp.float32)]
  transfers between devices with their start and end apart: 3 -> 0, of which waited for: 3 -> 0; matrix products, arithmetic and copies ran while one was open for 1% -> 0% of each run, Pallas kernels for 0% -> 0%
where the time goes in v4:
time: 86.9 us; the launch traced here: 86.5 us
  Pallas kernels  77.3 us (89%)
  local copies, waits for them, and re-layouts  6.25 us (7%)
  other arithmetic  2.18 us (3%)
    pallas_call x1, Pallas kernels, exchange(): pl.pallas_call(kernel, out_shape=(out, out), in_specs=[vmem, vmem], out_s...  77.3 us

profile of v4, /device:TPU:4, one launch (start us, length us, event | category | flops | bytes accessed | tf_op | source)
XLA Modules:
  0.0 86.5 jit_solution(821748682370999163)
XLA Ops:
  0.6 0.8 dynamic_slice.14
  1.4 0.8 broadcast_multiply_fusion
  2.2 0.8 dynamic_slice.13
  3.0 0.8 dynamic_slice.15
  3.7 0.0 copy-start.1
  3.7 1.3 %reshape.28 = bf16[4,158,512]{2,1,0:T(8,128)(2,1)S(1)} reshape(bf16[632,4,128]{2,1,0:T(4,128)(2,1)} %param.4) | data formatting | bytes 1294336 | tf_op jit(solution)/shard_map/reshape | solution.py:426
  5.1 0.1 slice.26
  5.1 0.0 copy-done.1
  5.2 0.1 slice_select_fusion
  5.3 0.0 copy-start
  5.4 1.0 %copy-done = bf16[632,4,128]{2,1,0:T(4,128)(2,1)S(1)} copy-done((bf16[632,4,128]{2,1,0:T(4,128)(2,1)S(1)}, bf16[632,4,128]{2,1,0:T(4,128)(2,1)}, u32[]{:S(2)}) %copy-start) | copy-done | bytes 647192
  6.4 0.2 reshape.31
  6.6 0.1 pad.14.g_ref
  6.7 77.3 %shard_map.59 = (f32[4,160,256]{2,1,0:T(8,128)S(1)}, f32[4,160,256]{2,1,0:T(8,128)S(1)}) custom-call(bf16[640,512]{1,0:T(8,128)(2,1)S(1)} %pad_maximum_fusion.s_ref, bf16[4,160,512]{2,1,0:T(8,128)(2,1)S(1)} %pad.14.g_ref), custom_call_target="tpu_custom_call" | custom-call | flops 3355443200 | bytes 4194304 | tf_op jit(solution)/shard_map/pallas_call | solution.py:398
  84.1 0.1 maximum_bitcast_fusion
  84.2 0.4 copy.7
  84.6 0.4 reshape.32
  85.0 0.1 pad_maximum_fusion.1
  85.1 0.1 reshape.34
  85.2 0.2 copy.9
  85.4 1.2 %add_divide_fusion = (f32[158,632]{1,0:T(8,128)}, f32[158,632]{1,0:T(8,128)}) fusion(f32[632]{0:T(1024)S(1)} %dynamic_slice.15, f32[158]{0:T(256)S(1)} %dynamic_slice.14, s32[158]{0:T(256)S(1)} %get-tuple-element.8, s32[632]{0:T(1024)S(1)} %dynamic_slice.13, s32[158]{0:T(256)S(1)} %get-tuple-element.9, f32[158,632]{1,0:T(8,128)S(1)} %reshape.32, ...), kind=kLoop, calls=%fused_computation.5 | loop fusion | flops 1298128 | bytes 1604648 | tf_op jit(solution)/shard_map/div | solution.py:445
  (6 shorter events, 0.2 us)
Async XLA Ops:
  3.7 1.4 %copy-start.1 = (pred[96]{0:T(512)(128)(4,1)S(1)}, pred[96]{0:T(512)(128)(4,1)}, u32[]{:S(2)}) copy-start(pred[96]{0:T(512)(128)(4,1)} %constant.7.clone.1) | copy-start | bytes 292
  5.3 1.1 %copy-start = (bf16[632,4,128]{2,1,0:T(4,128)(2,1)S(1)}, bf16[632,4,128]{2,1,0:T(4,128)(2,1)}, u32[]{:S(2)}) copy-start(bf16[632,4,128]{2,1,0:T(4,128)(2,1)} %param.5) | copy-start | bytes 1941508

commit v5 on v4

--- a/solution.py
+++ b/solution.py
@@ -61,7 +61,7 @@
     return jnp.concatenate(parts, axis=0)
 
 
-def kernel(s_ref, g_ref, direct, mirror, sbuf, gbuf, fock, *rest):
+def kernel(s_raw, g_raw, levels, gradient, rotation, direct, mirror, weight, g_ref, sbuf, gbuf, fock, *rest):
     n = len(GROUPS)
     outgoing, incoming, rest = rest[:n], rest[n:2 * n], rest[2 * n:]
     reduced, packed, direct_codes, mirror_codes, by_y, by_x = (rest[2 * i:2 * i + 2] for i in range(6))
@@ -162,27 +162,31 @@
         for p in range(4):
             got(cross[d][p], piece(1 - c, d, p), other)
 
-    s_out = [slots(5) for _ in ROWS]
-
-    def chunk_rows(h):
-        return pl.ds(4 * FIRST[h], 4 * ROWS[h])
+    s_out, s_far = [slots(4) for _ in ROWS], [slots(2) for _ in ROWS]
 
     def half_rows(h, i):
         return pl.ds(4 * FIRST[h] + 2 * ROWS[h] * i, 2 * ROWS[h])
 
     def send_rows(h):
-        for d in (1, 3):
-            put(s_out[h][d], s_ref.at[chunk_rows(h)], sbuf.at[chunk_rows(h), lanes[4 - d]], x_at(d))
+        for part in range(2):
+            for i, d in enumerate((1, 3)):
+                rows = half_rows(h, (i + part) % 2)
+                put(s_out[h][2 * i + part], sbuf.at[rows, lanes[0]], sbuf.at[rows, lanes[4 - d]], x_at(d))
+
+    def near_rows(h, part):
+        for i, d in enumerate((1, 3)):
+            rows = half_rows(h, (i + part) % 2)
+            got(s_out[h][2 * i + part], sbuf.at[rows, lanes[4 - d]], x_at(4 - d))
+            if part == 0:
+                put(s_far[h][i], sbuf.at[rows, lanes[4 - d]], sbuf.at[rows, lanes[2]], x_at(d))
 
     def forward_rows(h):
+        near_rows(h, 0)
+
+    def finish_rows(h):
+        near_rows(h, 1)
         for i, d in enumerate((1, 3)):
-            got(s_out[h][d], sbuf.at[chunk_rows(h), lanes[4 - d]], x_at(4 - d))
-            put(s_out[h][2 * i + 2], sbuf.at[half_rows(h, i), lanes[4 - d]],
-                sbuf.at[half_rows(h, i), lanes[2]], x_at(d))
-
-    def finish_rows(h):
-        for i, d in enumerate((1, 3)):
-            got(s_out[h][2 * i + 2], sbuf.at[half_rows(h, i), lanes[2]], x_at(4 - d))
+            got(s_far[h][i], sbuf.at[half_rows(h, i), lanes[2]], x_at(4 - d))
 
     def multiply(h, core, near, far):
         a = sbuf[4 * FIRST[h]:4 * (FIRST[h] + ROWS[h])]
@@ -320,20 +324,56 @@
 
         lax.fori_loop(0, 4, one, 0)
 
+    def flat(ref, first, rows):
+        return ref[first:first + rows].reshape(rows, KX)
+
+    block = s_raw.shape[0] // 4
+    for m in range(4):
+        g_ref[m, SUB - 16:SUB] = jnp.zeros((16, KX), jnp.bfloat16)
+        g_ref[m, 0:block] = flat(g_raw, block * m, block)
+    def window(first, size):
+        wide = LANES * (size // LANES + 2)
+        base = pl.multiple_of(first // LANES * LANES, LANES)
+        return pltpu.roll(levels[:, pl.ds(base, wide)], (wide - first % LANES) % wide, 1)
+
+    def weigh():
+        n = 4 * block
+        across = window(n * col, n)[:, :n]
+        down = window(block * (4 * row + aux), block)[:, :2 * LANES].T[:block]
+        occupied, filled = down[:, 1:2], across[1:2]
+        pairs = occupied + filled - 2.0 * occupied * filled
+        weight[...] = -pairs / (4.0 * jnp.abs(down[:, 0:1] - across[0:1]) + 0.5)
+
+    def finish():
+        lines = [slice(FIRST[h], FIRST[h] + min(ROWS[h] - 1, block - FIRST[h] + h)) for h in range(2)]
+        mine = jnp.concatenate([direct[m, :, :block] for m in range(4)], axis=1)
+        turned = [mirror[r].T[:block] for r in range(4)]
+        theirs = jnp.concatenate([t[:, part] for t in turned for part in lines], axis=1)
+        mine = jnp.concatenate([mine[part] for part in lines], axis=0)
+        total = 2.0 * (mine - theirs)
+        gradient[...] = total
+        rotation[...] = weight[...] * total
+
     for d in (1, 3, 2):
         put(a2a[d], g_ref.at[(x + d) % 4], piece(c, 0, 4 - d), x_at(d))
     gbuf[c, 0, :, 0:KX] = g_ref[x]
     spread(0)
-    sbuf[:, 0:KX] = s_ref[...]
+    for h in range(2):
+        rows = min(ROWS[h] - 1, block - FIRST[h] + h)
+        for r in range(4):
+            first = 4 * FIRST[h] + ROWS[h] * r
+            sbuf[first + ROWS[h] - 16:first + ROWS[h], 0:KX] = jnp.zeros((16, KX), jnp.bfloat16)
+            sbuf[first:first + rows, 0:KX] = flat(s_raw, block * r + FIRST[h] - h, rows)
     arrived(1)
     arrived(3)
     send_rows(0)
+    weigh()
     relay(0)
     arrived(2)
     relay(3)
-    relay(1)
     forward_rows(0)
     send_rows(1)
+    relay(1)
     relay(2)
     for d in (0, 1, 3):
         crossed(d)
@@ -361,9 +401,9 @@
     own(0)
     hop(2, 2)
     hop(1, 3)
+    hop(2, 3)
     own(1)
     leave(0)
-    hop(2, 3)
     turn(0)
     own(2)
     leave(1)
@@ -374,6 +414,7 @@
     unpack(0)
     arrive(1)
     unpack(1)
+    finish()
     for copy in sends:
         copy.wait_send()
     for h in range(2):
@@ -387,20 +428,25 @@
                 along_z(h, m).wait_send()
 
 
-COPIES = 4 + 16 + 16 + 10 + 7 * len(GROUPS) + 32
-
-
-def exchange(slabs, gammas):
+COPIES = 4 + 16 + 16 + 12 + 7 * len(GROUPS) + 32
+
+
+def exchange(slabs, gammas, levels):
     vmem = pl.BlockSpec(memory_space=pltpu.VMEM)
-    out = jax.ShapeDtypeStruct((4, SUB, 2 * LANES), jnp.float32)
+    block = slabs.shape[0]
+    out = jax.ShapeDtypeStruct((block // 4, block), jnp.float32)
     hops = [pltpu.VMEM((2, 4, ROWS[h], last - first), jnp.int16) for h, first, last, _ in GROUPS]
     pieces = [pltpu.VMEM((4, p, LANES), jnp.int16) for p in PACKED]
     return pl.pallas_call(
         kernel,
         out_shape=(out, out),
-        in_specs=[vmem, vmem],
+        in_specs=[vmem, vmem, vmem],
         out_specs=(vmem, vmem),
         scratch_shapes=[
+            pltpu.VMEM((4, SUB, 2 * LANES), jnp.float32),
+            pltpu.VMEM((4, SUB, 2 * LANES), jnp.float32),
+            pltpu.VMEM((block // 4, block), jnp.float32),
+            pltpu.VMEM((4, SUB, KX), jnp.bfloat16),
             pltpu.VMEM((4 * SUB, 4 * KX), jnp.bfloat16),
             pltpu.VMEM((2, 4, SUB, 4 * KX), jnp.bfloat16),
             pltpu.VMEM((4, 2, SUB, WIDE), jnp.float32),
@@ -415,35 +461,13 @@
             collective_id=0, has_side_effects=True, vmem_limit_bytes=48 * 1024 * 1024),
         cost_estimate=pl.CostEstimate(
             flops=2 * 640 * 1280 * 2048, bytes_accessed=4 * 1024 * 1024, transcendentals=0),
-    )(slabs, gammas)
+    )(slabs, gammas, levels)
 
 
 def on_device(slabs, gammas, occupied, energies):
-    block = slabs.shape[0]
-    sub = block // 4
-    row, col, aux = lax.axis_index("row"), lax.axis_index("col"), lax.axis_index("aux")
-    split = ROWS[0] - 1
-    rows = slabs.reshape(4, sub, KX)
-    parts = [jnp.pad(part, ((0, 0), (0, 1), (0, 0))).reshape(-1, KX) for part in (rows[:, :split], rows[:, split:])]
-    g = jnp.pad(gammas.reshape(4, sub, KX), ((0, 0), (0, SUB - sub), (0, 0)))
-    direct, mirror = exchange(jnp.concatenate(parts), g)
-
-    def trim(a):
-        return jnp.concatenate([a[:, :split, :sub], a[:, split + 1:SUB - 1, :sub]], axis=1)
-
-    own = trim(direct).transpose(1, 0, 2).reshape(sub, block)
-    other = trim(mirror).reshape(block, sub).T
-    gradient = 2.0 * (own - other)
-    row_start = row * block + aux * sub
-    col_start = col * block
-    energy_rows = lax.dynamic_slice_in_dim(energies, row_start, sub)
-    energy_cols = lax.dynamic_slice_in_dim(energies, col_start, block)
-    occ_rows = lax.dynamic_slice_in_dim(occupied, row_start, sub)
-    occ_cols = lax.dynamic_slice_in_dim(occupied, col_start, block)
-    nonredundant = occ_rows[:, None] + occ_cols[None, :] - 2 * occ_rows[:, None] * occ_cols[None, :]
-    denominator = 4.0 * jnp.abs(energy_rows[:, None] - energy_cols[None, :]) + 0.5
-    rotation_step = -nonredundant.astype(jnp.float32) * gradient / denominator
-    return (gradient, rotation_step)
+    rows = jnp.stack([energies, occupied.astype(jnp.float32)])
+    tail = -rows.shape[1] % LANES + 2 * LANES
+    return exchange(slabs, gammas, jnp.pad(rows, ((0, 6), (0, tail))))
 
 
 def solution(mesh):

time: 86.9 us -> 82.2 us (0.946)
  local copies, waits for them, and re-layouts: 6.25 us -> 3.67 us
  other arithmetic: 2.18 us -> 0.79 us
    unnamed x4 -> x8, local copies, waits for them, and re-layouts: 1.03 us -> 3.67 us
    dynamic_slice x3 -> x0, local copies, waits for them, and re-layouts: 2.32 us -> none  [the longest x1 0.78 us: on_device(): energy_rows = lax.dynamic_slice_in_dim(energies, row_start, sub)]
    reshape x5 -> x0, local copies, waits for them, and re-layouts: 2.25 us -> none  [the longest x1 1.34 us: on_device(): rows = slabs.reshape(4, sub, KX)]
    div x1 -> x0, other arithmetic: 1.15 us -> none  [on_device(): rotation_step = -nonredundant.astype(jnp.float32) * gradient / denominator]
where the time goes in v5:
time: 82.2 us; the launch traced here: 82 us
  Pallas kernels  76.9 us (94%)
  local copies, waits for them, and re-layouts  3.67 us (4%)
    pallas_call x1, Pallas kernels, exchange(): pl.pallas_call(kernel, out_shape=(out, out), in_specs=[vmem, vmem, vmem],...  76.9 us
    unnamed x8, local copies, waits for them, and re-layouts  3.67 us

profile of v5, /device:TPU:4, one launch (start us, length us, event | category | flops | bytes accessed | tf_op | source)
XLA Modules:
  0.0 82.0 jit_solution(8145270569263538362)
XLA Ops:
  0.6 0.0 copy-start.2
  0.6 0.7 convert_element_type.5
  1.4 0.0 copy-done.2
  1.4 0.1 select_maximum_fusion.levels
  1.4 0.0 copy-start
  1.4 1.1 %copy-done = bf16[632,4,128]{2,1,0:T(4,128)(2,1)S(1)} copy-done((bf16[632,4,128]{2,1,0:T(4,128)(2,1)S(1)}, bf16[632,4,128]{2,1,0:T(4,128)(2,1)}, u32[]{:S(2)}) %copy-start) | copy-done | bytes 647192
  2.5 0.0 copy-start.1
  2.5 1.1 %copy-done.1 = bf16[632,4,128]{2,1,0:T(4,128)(2,1)S(1)} copy-done((bf16[632,4,128]{2,1,0:T(4,128)(2,1)S(1)}, bf16[632,4,128]{2,1,0:T(4,128)(2,1)}, u32[]{:S(2)}) %copy-start.1) | copy-done | bytes 647192
  3.6 76.9 %shard_map.59 = (f32[158,632]{1,0:T(8,128)S(1)}, f32[158,632]{1,0:T(8,128)S(1)}) custom-call(bf16[632,4,128]{2,1,0:T(4,128)(2,1)S(1)} %copy-done, bf16[632,4,128]{2,1,0:T(4,128)(2,1)S(1)} %copy-done.1, f32[8,5376]{1,0:T(8,128)S(1)} %select_maximum_fusion.levels), custom_call_target="tpu_custom_call" | custom-call | flops 3355443200 | bytes 4194304 | tf_op jit(solution)/shard_map/pallas_call | solution.py:440
  80.5 0.8 copy.8
  81.2 0.8 copy.9
Async XLA Ops:
  0.6 0.7 copy-start.2
  1.4 1.1 %copy-start = (bf16[632,4,128]{2,1,0:T(4,128)(2,1)S(1)}, bf16[632,4,128]{2,1,0:T(4,128)(2,1)}, u32[]{:S(2)}) copy-start(bf16[632,4,128]{2,1,0:T(4,128)(2,1)} %s_raw.1) | copy-start | bytes 1941508
  2.5 1.1 %copy-start.1 = (bf16[632,4,128]{2,1,0:T(4,128)(2,1)S(1)}, bf16[632,4,128]{2,1,0:T(4,128)(2,1)}, u32[]{:S(2)}) copy-start(bf16[632,4,128]{2,1,0:T(4,128)(2,1)} %g_raw.1) | copy-start | bytes 1941508

commit v6 on v5

--- a/solution.py
+++ b/solution.py
@@ -18,6 +18,7 @@
 FINE = 128.0
 PLACE = (0, 1, 3, 2)
 GROUPS = ((0, 0, 3 * LANES, 1), (0, 3 * LANES, WIDE, 1), (1, 0, WIDE, 0))
+SHORT = (1, 2)
 MESH = pl.DeviceIdType.MESH
 
 
@@ -61,12 +62,17 @@
     return jnp.concatenate(parts, axis=0)
 
 
-def kernel(s_raw, g_raw, levels, gradient, rotation, direct, mirror, weight, g_ref, sbuf, gbuf, fock, *rest):
+def kernel(s_hbm, g_hbm, energies, occupied, gradient, weight, levels, direct, mirror, s_raw, g_raw, g_ref, sbuf, gbuf, fock, *rest):
     n = len(GROUPS)
     outgoing, incoming, rest = rest[:n], rest[n:2 * n], rest[2 * n:]
     reduced, packed, direct_codes, mirror_codes, by_y, by_x = (rest[2 * i:2 * i + 2] for i in range(6))
     send, recv, loc = rest[12:]
 
+    fetch = [pltpu.make_async_copy(src, dst, loc.at[8 + i])
+             for i, (src, dst) in enumerate(((g_hbm, g_raw), (s_hbm, s_raw)))]
+    for copy in fetch:
+        copy.start()
+
     row, col, aux = lax.axis_index("row"), lax.axis_index("col"), lax.axis_index("aux")
     y, c = row // 2, row % 2
     x, zlo = col // 2, col % 2
@@ -96,14 +102,12 @@
     def greet(dev):
         pl.semaphore_signal(barrier, inc=1, device_id=dev, device_id_type=MESH)
 
-    for dev in (x_at(1), x_at(3), x_at(2), y_at(1), y_at(3), y_at(2), other, z_at(1), z_at(7)):
+    for dev in (x_at(1), x_at(3), x_at(2), y_at(1), y_at(3), y_at(2), other, z_at(1), z_at(7), z_at(2), z_at(6)):
         greet(dev)
     for r in range(4):
         @pl.when(jnp.logical_not(jnp.logical_and(same_core, aux == r)))
         def _():
             greet(swapped(r))
-
-    pl.semaphore_wait(barrier, 13 - same_core.astype(jnp.int32))
 
     sends = []
     count = [0]
@@ -230,15 +234,50 @@
                 outgoing[k][way, step, :, cols] = encode(v)
             put(rs[k][way][step], outgoing[k].at[way, step], incoming[k].at[way, step], z_at(sign))
 
+    AWAY = (3, 1, 2, 4)
+    REACH = (1, 1, 2, 2)
+
+    def message(k, way, n, others):
+        sign = 1 if way == 0 else 7
+        for i in tiles(k):
+            cols = pl.ds(LANES * i, LANES)
+            v = fock[sums(k, sign * AWAY[n], i)]
+            for m in others:
+                v += decode(incoming[k][way, m, :, cols])
+            outgoing[k][way, n, :, cols] = encode(v)
+        put(rs[k][way][n], outgoing[k].at[way, n], incoming[k].at[way, n], z_at(sign * REACH[n]))
+
+    def came(k, way, n):
+        sign = 1 if way == 0 else 7
+        got(rs[k][way][n], incoming[k].at[way, n], z_at((8 - sign) * REACH[n]))
+
+    def begin(k):
+        for n in (3, 0, 1):
+            for way in range(2):
+                if n < len(rs[k][way]):
+                    message(k, way, n, ())
+
+    def meet(k):
+        for way in (1, 0):
+            others = (0, 3) if len(rs[k][way]) == 4 else (0,)
+            for n in others:
+                came(k, way, n)
+            message(k, way, 2, others)
+
     def own(k):
         h, first, _, _ = GROUPS[k]
+        last = [(1, 2) if k in SHORT else (len(rs[k][way]) - 1,) for way in range(2)]
         for way in range(2):
-            hops = len(rs[k][way])
-            got(rs[k][way][-1], incoming[k].at[way, hops - 1], z_at(7 if way == 0 else 1))
+            for n in last[way]:
+                if k in SHORT:
+                    came(k, way, n)
+                else:
+                    got(rs[k][way][n], incoming[k].at[way, n], z_at(7 if way == 0 else 1))
         for i in tiles(k):
             v = fock[sums(k, 0, i)]
             for way in range(2):
-                v += decode(incoming[k][way, len(rs[k][way]) - 1, :, pl.ds(LANES * i, LANES)])
+                for n in last[way]:
+                    v += decode(incoming[k][way, n, :, pl.ds(LANES * i, LANES)])
             reduced[h][:, first + LANES * i:first + LANES * (i + 1)] = encode(v)
 
     x_out, y_out = [slots(4) for _ in ROWS], [slots(4) for _ in ROWS]
@@ -328,20 +367,26 @@
         return ref[first:first + rows].reshape(rows, KX)
 
     block = s_raw.shape[0] // 4
+    fetch[0].wait()
     for m in range(4):
         g_ref[m, SUB - 16:SUB] = jnp.zeros((16, KX), jnp.bfloat16)
         g_ref[m, 0:block] = flat(g_raw, block * m, block)
+    pl.semaphore_wait(barrier, 15 - same_core.astype(jnp.int32))
+
     def window(first, size):
         wide = LANES * (size // LANES + 2)
         base = pl.multiple_of(first // LANES * LANES, LANES)
         return pltpu.roll(levels[:, pl.ds(base, wide)], (wide - first % LANES) % wide, 1)
 
     def weigh():
+        levels[...] = jnp.zeros_like(levels)
+        levels[0:1, 0:energies.shape[1]] = energies[...]
+        levels[1:2, 0:energies.shape[1]] = occupied[...].astype(jnp.float32)
         n = 4 * block
         across = window(n * col, n)[:, :n]
         down = window(block * (4 * row + aux), block)[:, :2 * LANES].T[:block]
-        occupied, filled = down[:, 1:2], across[1:2]
-        pairs = occupied + filled - 2.0 * occupied * filled
+        full, filled = down[:, 1:2], across[1:2]
+        pairs = full + filled - 2.0 * full * filled
         weight[...] = -pairs / (4.0 * jnp.abs(down[:, 0:1] - across[0:1]) + 0.5)
 
     def finish():
@@ -350,14 +395,13 @@
         turned = [mirror[r].T[:block] for r in range(4)]
         theirs = jnp.concatenate([t[:, part] for t in turned for part in lines], axis=1)
         mine = jnp.concatenate([mine[part] for part in lines], axis=0)
-        total = 2.0 * (mine - theirs)
-        gradient[...] = total
-        rotation[...] = weight[...] * total
+        gradient[...] = mine - theirs
 
     for d in (1, 3, 2):
         put(a2a[d], g_ref.at[(x + d) % 4], piece(c, 0, 4 - d), x_at(d))
     gbuf[c, 0, :, 0:KX] = g_ref[x]
     spread(0)
+    fetch[1].wait()
     for h in range(2):
         rows = min(ROWS[h] - 1, block - FIRST[h] + h)
         for r in range(4):
@@ -383,32 +427,28 @@
     hop(0, 0)
     for p in (0, 3, 1, 2):
         relay_far(p)
+    forward_rows(1)
     multiply(0, c, False, True)
-    forward_rows(1)
-    hop(0, 1)
     crossed(2)
     multiply(0, 1 - c, False, True)
-    hop(1, 0)
-    hop(0, 2)
+    begin(1)
+    hop(0, 1)
     finish_rows(1)
     multiply(1, c, True, True)
     multiply(1, 1 - c, True, True)
-    hop(2, 0)
-    hop(1, 1)
+    begin(2)
+    hop(0, 2)
+    meet(1)
     hop(0, 3)
-    hop(2, 1)
-    hop(1, 2)
+    meet(2)
     own(0)
-    hop(2, 2)
-    hop(1, 3)
-    hop(2, 3)
     own(1)
     leave(0)
-    turn(0)
     own(2)
     leave(1)
+    turn(0)
+    turn(1)
     swap(0)
-    turn(1)
     swap(1)
     arrive(0)
     unpack(0)
@@ -431,8 +471,8 @@
 COPIES = 4 + 16 + 16 + 12 + 7 * len(GROUPS) + 32
 
 
-def exchange(slabs, gammas, levels):
-    vmem = pl.BlockSpec(memory_space=pltpu.VMEM)
+def exchange(slabs, gammas, energies, occupied):
+    vmem, hbm = pl.BlockSpec(memory_space=pltpu.VMEM), pl.BlockSpec(memory_space=pltpu.HBM)
     block = slabs.shape[0]
     out = jax.ShapeDtypeStruct((block // 4, block), jnp.float32)
     hops = [pltpu.VMEM((2, 4, ROWS[h], last - first), jnp.int16) for h, first, last, _ in GROUPS]
@@ -440,12 +480,14 @@
     return pl.pallas_call(
         kernel,
         out_shape=(out, out),
-        in_specs=[vmem, vmem, vmem],
+        in_specs=[hbm, hbm, vmem, vmem],
         out_specs=(vmem, vmem),
         scratch_shapes=[
+            pltpu.VMEM((8, -(-energies.shape[1] // LANES) * LANES + 2 * LANES), jnp.float32),
             pltpu.VMEM((4, SUB, 2 * LANES), jnp.float32),
             pltpu.VMEM((4, SUB, 2 * LANES), jnp.float32),
-            pltpu.VMEM((block // 4, block), jnp.float32),
+            pltpu.VMEM(slabs.shape, slabs.dtype),
+            pltpu.VMEM(gammas.shape, gammas.dtype),
             pltpu.VMEM((4, SUB, KX), jnp.bfloat16),
             pltpu.VMEM((4 * SUB, 4 * KX), jnp.bfloat16),
             pltpu.VMEM((2, 4, SUB, 4 * KX), jnp.bfloat16),
@@ -455,19 +497,19 @@
             *pieces, *pieces, *pieces, *pieces, *pieces,
             pltpu.SemaphoreType.DMA((COPIES,)),
             pltpu.SemaphoreType.DMA((COPIES,)),
-            pltpu.SemaphoreType.DMA((8,)),
+            pltpu.SemaphoreType.DMA((10,)),
         ],
         compiler_params=pltpu.CompilerParams(
-            collective_id=0, has_side_effects=True, vmem_limit_bytes=48 * 1024 * 1024),
+            collective_id=0, has_side_effects=True, vmem_limit_bytes=53 * 1024 * 1024),
         cost_estimate=pl.CostEstimate(
             flops=2 * 640 * 1280 * 2048, bytes_accessed=4 * 1024 * 1024, transcendentals=0),
-    )(slabs, gammas, levels)
+    )(slabs, gammas, energies, occupied)
 
 
 def on_device(slabs, gammas, occupied, energies):
-    rows = jnp.stack([energies, occupied.astype(jnp.float32)])
-    tail = -rows.shape[1] % LANES + 2 * LANES
-    return exchange(slabs, gammas, jnp.pad(rows, ((0, 6), (0, tail))))
+    half, weight = exchange(slabs, gammas, energies[None], occupied[None])
+    gradient = 2.0 * half
+    return gradient, weight * gradient
 
 
 def solution(mesh):

time: 82.2 us -> 79.4 us (0.966); the launches traced: 82 us -> 78.3 us
  local copies, waits for them, and re-layouts: 3.67 us -> 1.45 us
  Pallas kernels: 76.9 us -> 75.3 us
    unnamed x8 -> x4, local copies, waits for them, and re-layouts: 3.67 us -> 1.45 us
    pallas_call x1, Pallas kernels: 76.9 us -> 75.3 us  [exchange(): pl.pallas_call(kernel, out_shape=(out, out), in_specs=[hbm, hbm, vmem, vm...]
    mul x0 -> x1, other arithmetic: none -> 0.94 us  [on_device(): return (gradient, weight * gradient)]
where the time goes in v6:
time: 79.4 us; the launch traced here: 78.3 us
  Pallas kernels  75.3 us (95%)
  local copies, waits for them, and re-layouts  1.45 us (2%)
  other arithmetic  0.94 us (1%)
    pallas_call x1, Pallas kernels, exchange(): pl.pallas_call(kernel, out_shape=(out, out), in_specs=[hbm, hbm, vmem, vm...  75.3 us

profile of v6, /device:TPU:4, one launch (start us, length us, event | category | flops | bytes accessed | tf_op | source)
XLA Modules:
  0.0 78.3 jit_solution(2730927790696509756)
XLA Ops:
  0.6 0.0 copy-start
  0.6 0.7 copy-done
  1.4 0.0 copy-start.1
  1.4 0.7 copy-done.1
  2.1 75.3 %shard_map.59 = (f32[158,632]{1,0:T(8,128)S(1)}, f32[158,632]{1,0:T(8,128)S(1)}) custom-call(bf16[632,4,128]{2,1,0:T(4,128)(2,1)} %s_hbm.1, bf16[632,4,128]{2,1,0:T(4,128)(2,1)} %g_hbm.1, f32[1,5056]{1,0:T(1,128)S(1)} %bitcast.2, s32[1,5056]{1,0:T(1,128)S(1)} %bitcast.3), custom_call_target="tpu_custom_call" | custom-call | flops 3355443200 | bytes 4194304 | tf_op jit(solution)/shard_map/pallas_call | solution.py:480
  77.4 0.9 %fusion = (f32[158,632]{1,0:T(8,128)}, f32[158,632]{1,0:T(8,128)}) fusion(f32[158,632]{1,0:T(8,128)S(1)} %get-tuple-element.5, f32[158,632]{1,0:T(8,128)S(1)} %get-tuple-element.4), kind=kLoop, calls=%fused_computation.1 | loop fusion | flops 199712 | bytes 1597696 | tf_op jit(solution)/shard_map/mul | solution.py:512
Async XLA Ops:
  0.6 0.7 copy-start
  1.4 0.7 copy-start.1

commit v7 on v6

--- a/solution.py
+++ b/solution.py
@@ -431,13 +431,13 @@
     multiply(0, c, False, True)
     crossed(2)
     multiply(0, 1 - c, False, True)
+    hop(0, 1)
     begin(1)
-    hop(0, 1)
     finish_rows(1)
     multiply(1, c, True, True)
+    hop(0, 2)
     multiply(1, 1 - c, True, True)
     begin(2)
-    hop(0, 2)
     meet(1)
     hop(0, 3)
     meet(2)

time: 79.4 us -> 78.4 us (0.987)
  Pallas kernels: 75.3 us -> 74.2 us
    pallas_call x1, Pallas kernels: 75.3 us -> 74.2 us  [exchange(): pl.pallas_call(kernel, out_shape=(out, out), in_specs=[hbm, hbm, vmem, vm...]
where the time goes in v7:
time: 78.4 us; the launch traced here: 77.2 us
  Pallas kernels  74.2 us (95%)
  local copies, waits for them, and re-layouts  1.45 us (2%)
  other arithmetic  0.94 us (1%)
    pallas_call x1, Pallas kernels, exchange(): pl.pallas_call(kernel, out_shape=(out, out), in_specs=[hbm, hbm, vmem, vm...  74.2 us

profile of v7, /device:TPU:4, one launch (start us, length us, event | category | flops | bytes accessed | tf_op | source)
XLA Modules:
  0.0 77.2 jit_solution(11153038919355332310)
XLA Ops:
  0.6 0.0 copy-start
  0.6 0.7 copy-done
  1.4 0.0 copy-start.1
  1.4 0.7 copy-done.1
  2.1 74.2 %shard_map.59 = (f32[158,632]{1,0:T(8,128)S(1)}, f32[158,632]{1,0:T(8,128)S(1)}) custom-call(bf16[632,4,128]{2,1,0:T(4,128)(2,1)} %s_hbm.1, bf16[632,4,128]{2,1,0:T(4,128)(2,1)} %g_hbm.1, f32[1,5056]{1,0:T(1,128)S(1)} %bitcast.2, s32[1,5056]{1,0:T(1,128)S(1)} %bitcast.3), custom_call_target="tpu_custom_call" | custom-call | flops 3355443200 | bytes 4194304 | tf_op jit(solution)/shard_map/pallas_call | solution.py:480
  76.3 0.9 %fusion = (f32[158,632]{1,0:T(8,128)}, f32[158,632]{1,0:T(8,128)}) fusion(f32[158,632]{1,0:T(8,128)S(1)} %get-tuple-element.5, f32[158,632]{1,0:T(8,128)S(1)} %get-tuple-element.4), kind=kLoop, calls=%fused_computation.1 | loop fusion | flops 199712 | bytes 1597696 | tf_op jit(solution)/shard_map/mul | solution.py:512
Async XLA Ops:
  0.6 0.7 copy-start
  1.4 0.7 copy-start.1

commit v8 on v7

--- a/solution.py
+++ b/solution.py
@@ -62,7 +62,7 @@
     return jnp.concatenate(parts, axis=0)
 
 
-def kernel(s_hbm, g_hbm, energies, occupied, gradient, weight, levels, direct, mirror, s_raw, g_raw, g_ref, sbuf, gbuf, fock, *rest):
+def kernel(s_hbm, g_hbm, pairs, gradient, weight, levels, direct, mirror, s_raw, g_raw, g_ref, sbuf, gbuf, fock, *rest):
     n = len(GROUPS)
     outgoing, incoming, rest = rest[:n], rest[n:2 * n], rest[2 * n:]
     reduced, packed, direct_codes, mirror_codes, by_y, by_x = (rest[2 * i:2 * i + 2] for i in range(6))
@@ -294,14 +294,16 @@
             packed[h][d, ROWS[h]:PACKED[h]] = fold(shared, t, h).astype(jnp.int16)
             if d:
                 put(y_out[h][d], packed[h].at[d], by_y[h].at[y], y_at(d))
+        copy = local(4 * h, packed[h].at[0], by_y[h].at[y])
+        copy.start()
+        copy.wait()
+
+    def depart(h):
         for d in (2, 1, 3):
             put(x_out[h][d], packed[h].at[(x + d - y + 4) % 4], direct_codes[h].at[x], x_at(d))
-        copies = (local(4 * h, packed[h].at[0], by_y[h].at[y]),
-                  local(4 * h + 1, packed[h].at[(x - y + 4) % 4], direct_codes[h].at[x]))
-        for copy in copies:
-            copy.start()
-        for copy in copies:
-            copy.wait()
+        copy = local(4 * h + 1, packed[h].at[(x - y + 4) % 4], direct_codes[h].at[x])
+        copy.start()
+        copy.wait()
 
     def along_x(h, d):
         t = (y + d) % 4
@@ -380,14 +382,13 @@
 
     def weigh():
         levels[...] = jnp.zeros_like(levels)
-        levels[0:1, 0:energies.shape[1]] = energies[...]
-        levels[1:2, 0:energies.shape[1]] = occupied[...].astype(jnp.float32)
+        levels[0:2, 0:pairs.shape[1]] = pairs[...]
         n = 4 * block
         across = window(n * col, n)[:, :n]
         down = window(block * (4 * row + aux), block)[:, :2 * LANES].T[:block]
         full, filled = down[:, 1:2], across[1:2]
-        pairs = full + filled - 2.0 * full * filled
-        weight[...] = -pairs / (4.0 * jnp.abs(down[:, 0:1] - across[0:1]) + 0.5)
+        mixed = full + filled - 2.0 * full * filled
+        weight[...] = -mixed / (4.0 * jnp.abs(down[:, 0:1] - across[0:1]) + 0.5)
 
     def finish():
         lines = [slice(FIRST[h], FIRST[h] + min(ROWS[h] - 1, block - FIRST[h] + h)) for h in range(2)]
@@ -444,10 +445,12 @@
     own(0)
     own(1)
     leave(0)
+    depart(0)
     own(2)
     leave(1)
     turn(0)
     turn(1)
+    depart(1)
     swap(0)
     swap(1)
     arrive(0)
@@ -471,7 +474,7 @@
 COPIES = 4 + 16 + 16 + 12 + 7 * len(GROUPS) + 32
 
 
-def exchange(slabs, gammas, energies, occupied):
+def exchange(slabs, gammas, pairs):
     vmem, hbm = pl.BlockSpec(memory_space=pltpu.VMEM), pl.BlockSpec(memory_space=pltpu.HBM)
     block = slabs.shape[0]
     out = jax.ShapeDtypeStruct((block // 4, block), jnp.float32)
@@ -480,10 +483,10 @@
     return pl.pallas_call(
         kernel,
         out_shape=(out, out),
-        in_specs=[hbm, hbm, vmem, vmem],
+        in_specs=[hbm, hbm, vmem],
         out_specs=(vmem, vmem),
         scratch_shapes=[
-            pltpu.VMEM((8, -(-energies.shape[1] // LANES) * LANES + 2 * LANES), jnp.float32),
+            pltpu.VMEM((8, -(-pairs.shape[1] // LANES) * LANES + 2 * LANES), jnp.float32),
             pltpu.VMEM((4, SUB, 2 * LANES), jnp.float32),
             pltpu.VMEM((4, SUB, 2 * LANES), jnp.float32),
             pltpu.VMEM(slabs.shape, slabs.dtype),
@@ -503,11 +506,11 @@
             collective_id=0, has_side_effects=True, vmem_limit_bytes=53 * 1024 * 1024),
         cost_estimate=pl.CostEstimate(
             flops=2 * 640 * 1280 * 2048, bytes_accessed=4 * 1024 * 1024, transcendentals=0),
-    )(slabs, gammas, energies, occupied)
+    )(slabs, gammas, pairs)
 
 
 def on_device(slabs, gammas, occupied, energies):
-    half, weight = exchange(slabs, gammas, energies[None], occupied[None])
+    half, weight = exchange(slabs, gammas, jnp.stack([energies, occupied.astype(jnp.float32)]))
     gradient = 2.0 * half
     return gradient, weight * gradient
 

time: 78.4 us -> 78.6 us (level)
  the two profiles are of different devices: /device:TPU:4 before, /device:TPU:7 now
where the time goes in v8:
time: 78.6 us; the launch traced here: 78.4 us
  Pallas kernels  76.1 us (97%)
  other arithmetic  1.72 us (2%)
    pallas_call x1, Pallas kernels, exchange(): pl.pallas_call(kernel, out_shape=(out, out), in_specs=[hbm, hbm, vmem], o...  76.1 us

profile of v8, /device:TPU:7, one launch (start us, length us, event | category | flops | bytes accessed | tf_op | source)
XLA Modules:
  0.0 78.4 jit_solution(327665451985470014)
XLA Ops:
  0.6 0.0 copy-start
  0.6 0.7 convert_element_type.3
  1.4 0.0 copy-done
  1.4 76.1 %shard_map.59 = (f32[158,632]{1,0:T(8,128)S(1)}, f32[158,632]{1,0:T(8,128)S(1)}) custom-call(bf16[632,4,128]{2,1,0:T(4,128)(2,1)} %s_hbm.1, bf16[632,4,128]{2,1,0:T(4,128)(2,1)} %g_hbm.1, f32[2,5056]{1,0:T(2,128)S(1)} %pad_maximum_fusion.pairs), custom_call_target="tpu_custom_call" | custom-call | flops 3355443200 | bytes 4194304 | tf_op jit(solution)/shard_map/pallas_call | solution.py:483
  77.5 0.9 %fusion = (f32[158,632]{1,0:T(8,128)}, f32[158,632]{1,0:T(8,128)}) fusion(f32[158,632]{1,0:T(8,128)S(1)} %get-tuple-element.5, f32[158,632]{1,0:T(8,128)S(1)} %get-tuple-element.4), kind=kLoop, calls=%fused_computation.2 | loop fusion | flops 199712 | bytes 1597696 | tf_op jit(solution)/shard_map/mul | solution.py:515
  (1 shorter events, 0.0 us)
Async XLA Ops:
  0.6 0.7 copy-start
